TPU v7x, 32 devices: a whole 2x2x4 slice. The times are simulated.
32 devices in a mesh: dp: 8 (over z, y), seq: 4 (over x, core).
Axes of the slice: x: 2, y: 2, z: 4, core: 2. Of those that a mesh axis runs over, the one named last changes fastest.
Arguments:
- tokens: bfloat16 [16, 2048, 768], P('dp', 'seq'), may hold values from -6 to 6
- segment_ids: int32 [16, 2048], P('dp', 'seq'), may hold values from 0 to 7, as said below
- pair_ids: int32 [16, 8], P('dp'), may hold values from 0 to 63, as said below
- w_query: bfloat16 [768, 768], replicated, may hold values from -0.21875 to 0.21875
- w_key: bfloat16 [768, 768], replicated, may hold values from -0.0390625 to 0.0390625
- w_value: bfloat16 [768, 768], replicated, may hold values from -0.21875 to 0.21875
- w_out: bfloat16 [768, 768], replicated, may hold values from -1.75 to 1.75
- w_up: bfloat16 [768, 3072], replicated, may hold values from -0.21875 to 0.21875
- w_down: bfloat16 [3072, 768], replicated, may hold values from -0.109375 to 0.109375
- w_proj: bfloat16 [768, 768], replicated, may hold values from -0.21875 to 0.21875
- gain_attn: float32 [768], replicated, may hold values from 0.5 to 1.5
- gain_ffn: float32 [768], replicated, may hold values from 0.5 to 1.5
- rel_bias: float32 [32, 12], replicated, may hold values from -4 to 4
Outputs:
- mixed: bfloat16 [16, 2048, 768], P('dp', 'seq')
- loss: float32 [], replicated
- grad_tokens: float32 [16, 2048, 768], P('dp', 'seq')
- g_query: float32 [768, 768], P('dp', 'seq')
- g_key: float32 [768, 768], P('dp', 'seq')
- g_value: float32 [768, 768], P('dp', 'seq')
- g_out: float32 [768, 768], P('dp', 'seq')
- g_up: float32 [768, 3072], P('dp', 'seq')
- g_down: float32 [3072, 768], P('dp', 'seq')
- g_proj: float32 [768, 768], P('dp', 'seq')
- g_gain_attn: float32 [768], replicated
- g_gain_ffn: float32 [768], replicated
- g_rel_bias: float32 [32, 12], replicated
Inputs may be any that keep to these rules, and one draw needn't show every extreme that they name: `segment_ids`: in each row the ids never fall along the row, and every id of 0 to 7 occurs. `pair_ids`: each pair id belongs to exactly two segments among all the rows.
All inputs are finite; a program needn't handle non-finite values.
Results may differ from a plain program's by a relative error of at most 0.02.
Values may be sent and summed in bfloat16 or wider, within the bound.
A program may use at most 448 MiB of HBM per device.

v0:
```python
import jax
import jax.numpy as jnp
from jax import lax
from jax.sharding import PartitionSpec as P

EPS = 1e-06
LOGIT_SCALE = 20.0
LIMITS = (12, 16, 23, 32, 46, 64, 91)


def bucket_of(offset, half_count):
    distance = jnp.abs(offset)
    beyond = 8 + sum(((distance >= bound_at).astype(jnp.int32) for bound_at in LIMITS))
    nearby = jnp.where(distance < 8, distance, beyond)
    return nearby + half_count * (offset > 0).astype(jnp.int32)


def normed(inputs, gain_vec):
    return inputs * lax.rsqrt(jnp.mean(inputs * inputs, axis=-1, keepdims=True) + EPS) * gain_vec


def unit_rows(inputs):
    return inputs * lax.rsqrt(jnp.sum(inputs * inputs, axis=-1, keepdims=True) + EPS)


def gelu_exact(inputs):
    return jax.nn.gelu(inputs, approximate=False)


def bias_from(onehot, table):
    high_part = table.astype(jnp.bfloat16)
    rest = table - high_part.astype(jnp.float32)
    middle = rest.astype(jnp.bfloat16)
    low_part = (rest - middle.astype(jnp.float32)).astype(jnp.bfloat16)
    summed = jnp.einsum("qkb,bh->hqk", onehot, high_part, preferred_element_type=jnp.float32)
    summed = summed + jnp.einsum("qkb,bh->hqk", onehot, middle, preferred_element_type=jnp.float32)
    return summed + jnp.einsum("qkb,bh->hqk", onehot, low_part, preferred_element_type=jnp.float32)


def project(inputs, weight):
    return jnp.einsum("rtd,de->rte", inputs, weight, preferred_element_type=jnp.float32)


def back_project(grads_in, weight):
    return jnp.einsum("rte,de->rtd", grads_in, weight, preferred_element_type=jnp.float32)


def outer_sum(inputs, grads_in):
    return jnp.einsum("rtd,rte->de", inputs, grads_in, preferred_element_type=jnp.float32)


def on_device(
    tokens,
    segment_ids,
    pair_ids,
    w_query,
    w_key,
    w_value,
    w_out,
    w_up,
    w_down,
    w_proj,
    gain_attn,
    gain_ffn,
    rel_bias,
):
    row_count, tok_local, model_width = tokens.shape
    head_count = rel_bias.shape[1]
    head_width = model_width // head_count
    bucket_count = rel_bias.shape[0]
    slot_count = pair_ids.shape[1]
    seq_parts = lax.axis_size("seq")
    row_length = tok_local * seq_parts
    step_rows = min(row_count, max(1, 512 // tok_local))
    step_count = row_count // step_rows
    own_pos = lax.axis_index("seq") * tok_local + jnp.arange(tok_local, dtype=jnp.int32)
    every_pos = jnp.arange(row_length, dtype=jnp.int32)
    bucket_ids = jnp.arange(bucket_count, dtype=jnp.int32)
    bucket_fwd = bucket_of(every_pos[None, :] - own_pos[:, None], bucket_count // 2)
    onehot_fwd = (bucket_fwd[:, :, None] == bucket_ids[None, None, :]).astype(jnp.bfloat16)
    bias_fwd = bias_from(onehot_fwd, rel_bias)

    def blocked(tensor):
        return tensor.reshape((step_count, step_rows) + tensor.shape[1:])

    def by_heads(tensor):
        return tensor.reshape(tensor.shape[:2] + (head_count, head_width))

    def masked_scores(query_block, key_block, query_seg, key_seg, rel_add):
        raw_scores = jnp.einsum(
            "rqhd,rkhd->rhqk",
            by_heads(query_block),
            by_heads(key_block),
            preferred_element_type=jnp.float32,
        )
        same_seg = query_seg[:, None, :, None] == key_seg[:, None, None, :]
        return jnp.where(same_seg, raw_scores + rel_add[None], -1000000000.0)

    def forward_step(element):
        query_block, key_block, value_block, query_seg, key_seg = element
        scores = masked_scores(query_block, key_block, query_seg, key_seg, bias_fwd)
        top_score = jnp.max(scores, axis=-1, keepdims=True)
        log_total = top_score + jnp.log(
            jnp.sum(jnp.exp(scores - top_score), axis=-1, keepdims=True)
        )
        weights = jnp.exp(scores - log_total).astype(jnp.bfloat16)
        output = jnp.einsum(
            "rhqk,rkhd->rqhd", weights, by_heads(value_block), preferred_element_type=jnp.float32
        )
        return (output.reshape(output.shape[:2] + (model_width,)), log_total[..., 0])

    x_float = tokens.astype(jnp.float32)
    normed_one, norm_one_back = jax.vjp(normed, x_float, gain_attn)
    normed_one_b = normed_one.astype(jnp.bfloat16)
    query_rows = project(normed_one_b, w_query).astype(jnp.bfloat16)
    key_rows = project(normed_one_b, w_key).astype(jnp.bfloat16)
    value_rows = project(normed_one_b, w_value).astype(jnp.bfloat16)
    own_seg = segment_ids.astype(jnp.bfloat16)
    keys_all, values_all, seg_all = (
        lax.all_gather(key_rows, "seq", axis=1, tiled=True),
        lax.all_gather(value_rows, "seq", axis=1, tiled=True),
        lax.all_gather(own_seg, "seq", axis=1, tiled=True),
    )
    attended, log_totals = lax.map(
        forward_step,
        (
            blocked(query_rows),
            blocked(keys_all),
            blocked(values_all),
            blocked(own_seg),
            blocked(seg_all),
        ),
    )
    attended_b = attended.reshape(tokens.shape).astype(jnp.bfloat16)
    log_totals = log_totals.reshape(row_count, head_count, tok_local)
    hidden = x_float + project(attended_b, w_out)
    normed_two, norm_two_back = jax.vjp(normed, hidden, gain_ffn)
    normed_two_b = normed_two.astype(jnp.bfloat16)
    up_proj = project(normed_two_b, w_up)
    act_value, act_back = jax.vjp(gelu_exact, up_proj)
    act_b = act_value.astype(jnp.bfloat16)
    block_out = hidden + project(act_b, w_down)
    member = (
        segment_ids[:, None, :] == jnp.arange(slot_count, dtype=jnp.int32)[None, :, None]
    ).astype(jnp.float32)
    part_sums = jnp.einsum("rsl,rld->rsd", member, block_out, precision=lax.Precision.HIGHEST)
    part_counts = jnp.sum(member, axis=-1)
    seg_sums, counts = lax.psum((part_sums, part_counts), "seq")
    pooled_b = (
        (seg_sums / counts[..., None])
        .reshape(row_count * slot_count, model_width)
        .astype(jnp.bfloat16)
    )
    proj = jnp.dot(pooled_b, w_proj, preferred_element_type=jnp.float32)
    embed, embed_back = jax.vjp(unit_rows, proj)
    embed_b = embed.astype(jnp.bfloat16)
    pair_flat = pair_ids.reshape(-1)
    pair_code = jnp.stack([pair_flat // 128, pair_flat % 128], axis=1).astype(jnp.bfloat16)
    every_embed, every_code = (
        lax.all_gather(embed_b, "dp", axis=0, tiled=True),
        lax.all_gather(pair_code, "dp", axis=0, tiled=True),
    )
    every_pair = every_code[:, 0].astype(jnp.int32) * 128 + every_code[:, 1].astype(jnp.int32)
    count_all = every_embed.shape[0]
    own_index = lax.axis_index("dp") * embed_b.shape[0] + jnp.arange(
        embed_b.shape[0], dtype=jnp.int32
    )
    raw_scores = jnp.einsum("ip,jp->ij", embed_b, every_embed, preferred_element_type=jnp.float32)
    logits = LOGIT_SCALE * raw_scores
    self_mask = own_index[:, None] == jnp.arange(count_all, dtype=jnp.int32)[None, :]
    partner = (pair_flat[:, None] == every_pair[None, :]) & ~self_mask
    masked = jnp.where(self_mask, -1000000000.0, logits)
    top_score = jnp.max(masked, axis=-1, keepdims=True)
    log_total = top_score + jnp.log(jnp.sum(jnp.exp(masked - top_score), axis=-1, keepdims=True))
    positive = jnp.sum(jnp.where(partner, logits, 0.0), axis=-1)
    loss_part = jnp.sum(log_total[:, 0] - positive) / seq_parts
    chance = jnp.exp(masked - log_total)
    grad_raw = (LOGIT_SCALE * ((chance - partner.astype(jnp.float32)) / count_all)).astype(
        jnp.bfloat16
    )
    grad_own = jnp.dot(grad_raw, every_embed, preferred_element_type=jnp.float32)
    grad_spread = jnp.einsum("ij,ip->jp", grad_raw, embed_b, preferred_element_type=jnp.float32)
    grad_embed = grad_own + lax.psum_scatter(grad_spread, "dp", scatter_dimension=0, tiled=True)
    (grad_proj,) = embed_back(grad_embed)
    grad_proj_b = grad_proj.astype(jnp.bfloat16)
    grad_wproj = (
        jnp.einsum("sd,sp->dp", pooled_b, grad_proj_b, preferred_element_type=jnp.float32)
        / seq_parts
    )
    grad_pooled = jnp.einsum("sp,dp->sd", grad_proj_b, w_proj, preferred_element_type=jnp.float32)
    grad_pooled = grad_pooled.reshape(row_count, slot_count, model_width) / counts[..., None]
    grad_block = jnp.einsum("rsl,rsd->rld", member, grad_pooled, precision=lax.Precision.HIGHEST)
    grad_block_b = grad_block.astype(jnp.bfloat16)
    grad_wdown = outer_sum(act_b, grad_block_b)
    (grad_up,) = act_back(back_project(grad_block_b, w_down))
    grad_up_b = grad_up.astype(jnp.bfloat16)
    grad_wup = outer_sum(normed_two_b, grad_up_b)
    grad_hidden_norm, grad_gain_ffn = norm_two_back(back_project(grad_up_b, w_up))
    grad_hidden = grad_block + grad_hidden_norm
    grad_hidden_b = grad_hidden.astype(jnp.bfloat16)
    grad_wout = outer_sum(attended_b, grad_hidden_b)
    grad_att = back_project(grad_hidden_b, w_out).astype(jnp.bfloat16)

    def query_side(element):
        query_block, key_block, value_block, query_seg, key_seg, norm_block, grad_block_in = element
        scores = masked_scores(query_block, key_block, query_seg, key_seg, bias_fwd)
        weights = jnp.exp(scores - norm_block[..., None])
        grad_weights = jnp.einsum(
            "rqhd,rkhd->rhqk",
            by_heads(grad_block_in),
            by_heads(value_block),
            preferred_element_type=jnp.float32,
        )
        centre = jnp.sum(grad_weights * weights, axis=-1, keepdims=True)
        grad_scores = (weights * (grad_weights - centre)).astype(jnp.bfloat16)
        grad_q = jnp.einsum(
            "rhqk,rkhd->rqhd", grad_scores, by_heads(key_block), preferred_element_type=jnp.float32
        )
        grad_q = grad_q.reshape(query_block.shape[:2] + (model_width,))
        table_part = jnp.einsum(
            "rhqk,qkb->bh", grad_scores, onehot_fwd, preferred_element_type=jnp.float32
        )
        grad_k = jnp.einsum(
            "rhqk,rqhd->rkhd",
            grad_scores,
            by_heads(query_block),
            preferred_element_type=jnp.float32,
        )
        grad_v = jnp.einsum(
            "rhqk,rqhd->rkhd",
            weights.astype(jnp.bfloat16),
            by_heads(grad_block_in),
            preferred_element_type=jnp.float32,
        )
        return (
            grad_q,
            table_part,
            grad_k.reshape(key_block.shape[:2] + (model_width,)),
            grad_v.reshape(key_block.shape[:2] + (model_width,)),
        )

    query_items = (
        blocked(query_rows),
        blocked(keys_all),
        blocked(values_all),
        blocked(own_seg),
        blocked(seg_all),
        blocked(log_totals),
        blocked(grad_att),
    )
    grad_q, table_parts, grad_k_all, grad_v_all = lax.map(query_side, query_items)
    grad_key, grad_value = (
        lax.psum_scatter(
            grad_k_all.reshape(row_count, row_length, model_width).astype(jnp.bfloat16),
            "seq",
            scatter_dimension=1,
            tiled=True,
        ).astype(jnp.float32),
        lax.psum_scatter(
            grad_v_all.reshape(row_count, row_length, model_width).astype(jnp.bfloat16),
            "seq",
            scatter_dimension=1,
            tiled=True,
        ).astype(jnp.float32),
    )
    grad_query_b = grad_q.reshape(tokens.shape).astype(jnp.bfloat16)
    grad_key_b = grad_key.astype(jnp.bfloat16)
    grad_value_b = grad_value.astype(jnp.bfloat16)
    grad_wquery = outer_sum(normed_one_b, grad_query_b)
    grad_wkey = outer_sum(normed_one_b, grad_key_b)
    grad_wvalue = outer_sum(normed_one_b, grad_value_b)
    grad_normed_one = (
        back_project(grad_query_b, w_query)
        + back_project(grad_key_b, w_key)
        + back_project(grad_value_b, w_value)
    )
    grad_x_norm, grad_gain_attn = norm_one_back(grad_normed_one)
    grad_tokens = grad_hidden + grad_x_norm
    table_grad = jnp.sum(table_parts, axis=0)
    sum_q, sum_k, sum_v, sum_o, sum_up, sum_down, sum_proj = (
        lax.psum_scatter(
            grad_wquery.astype(jnp.bfloat16), "dp", scatter_dimension=0, tiled=True
        ).astype(jnp.float32),
        lax.psum_scatter(
            grad_wkey.astype(jnp.bfloat16), "dp", scatter_dimension=0, tiled=True
        ).astype(jnp.float32),
        lax.psum_scatter(
            grad_wvalue.astype(jnp.bfloat16), "dp", scatter_dimension=0, tiled=True
        ).astype(jnp.float32),
        lax.psum_scatter(
            grad_wout.astype(jnp.bfloat16), "dp", scatter_dimension=0, tiled=True
        ).astype(jnp.float32),
        lax.psum_scatter(
            grad_wup.astype(jnp.bfloat16), "dp", scatter_dimension=0, tiled=True
        ).astype(jnp.float32),
        lax.psum_scatter(
            grad_wdown.astype(jnp.bfloat16), "dp", scatter_dimension=0, tiled=True
        ).astype(jnp.float32),
        lax.psum_scatter(
            grad_wproj.astype(jnp.bfloat16), "dp", scatter_dimension=0, tiled=True
        ).astype(jnp.float32),
    )
    g_query, g_key, g_value, g_out, g_up, g_down, g_proj = (
        lax.psum_scatter(sum_q.astype(jnp.bfloat16), "seq", scatter_dimension=1, tiled=True).astype(
            jnp.float32
        ),
        lax.psum_scatter(sum_k.astype(jnp.bfloat16), "seq", scatter_dimension=1, tiled=True).astype(
            jnp.float32
        ),
        lax.psum_scatter(sum_v.astype(jnp.bfloat16), "seq", scatter_dimension=1, tiled=True).astype(
            jnp.float32
        ),
        lax.psum_scatter(sum_o.astype(jnp.bfloat16), "seq", scatter_dimension=1, tiled=True).astype(
            jnp.float32
        ),
        lax.psum_scatter(
            sum_up.astype(jnp.bfloat16), "seq", scatter_dimension=1, tiled=True
        ).astype(jnp.float32),
        lax.psum_scatter(
            sum_down.astype(jnp.bfloat16), "seq", scatter_dimension=1, tiled=True
        ).astype(jnp.float32),
        lax.psum_scatter(
            sum_proj.astype(jnp.bfloat16), "seq", scatter_dimension=1, tiled=True
        ).astype(jnp.float32),
    )
    loss_total, table_total, gain_one_total, gain_two_total = lax.psum(
        (loss_part, table_grad, grad_gain_attn, grad_gain_ffn), ("dp", "seq")
    )
    return (
        block_out.astype(jnp.bfloat16),
        loss_total / count_all,
        grad_tokens,
        g_query,
        g_key,
        g_value,
        g_out,
        g_up,
        g_down,
        g_proj,
        gain_one_total,
        gain_two_total,
        table_total,
    )


def solution(mesh):
    in_specs = (
        P("dp", "seq", None),
        P("dp", "seq"),
        P("dp", None),
        P(),
        P(),
        P(),
        P(),
        P(),
        P(),
        P(),
        P(),
        P(),
        P(),
    )
    out_specs = (
        P("dp", "seq", None),
        P(),
        P("dp", "seq", None),
        P("dp", "seq"),
        P("dp", "seq"),
        P("dp", "seq"),
        P("dp", "seq"),
        P("dp", "seq"),
        P("dp", "seq"),
        P("dp", "seq"),
        P(),
        P(),
        P(),
    )
    return jax.shard_map(
        on_device, mesh=mesh, in_specs=in_specs, out_specs=out_specs, check_vma=False
    )
```

profile of v0, /device:TPU:0, one launch (start us, length us, event | category | flops | bytes accessed | tf_op | source)
XLA Modules:
  0.0 1779.6 jit_solution(1479976740264564303)
XLA Ops:
  85.0 67.2 %fusion.20 = f32[12,512,2048]{2,0,1:T(8,128)} fusion(f32[12,512,2048]{2,0,1:T(8,128)} %fusion.17, f32[12,512,2048]{2,0,1:T(8,128)} %fusion.18, s32[512,2048]{1,0:T(8,128)} %copy.80, f32[32,12]{0,1:T(8,128)S(1)} %copy-done.23), kind=kOutput, calls=%fused_computation.43 | convolution fusion | flops 864027008 | bytes 155190784 | tf_op jit(solution)/shard_map/qkb,bh->hqk/dot_general | solution.py:35
  152.3 44.2 %copy.86 = f32[12,512,2048]{2,1,0:T(8,128)} copy(f32[12,512,2048]{2,0,1:T(8,128)} %fusion.20) | data formatting | bytes 100663296 | tf_op jit(solution)/shard_map/while | solution.py:124
  249.7 162.9 %while.29 = (s32[]{:T(128)}, bf16[2,1,512,768]{2,3,1,0:T(8,128)(2,1)}, f32[2,1,12,512]{3,2,1,0:T(8,128)}, bf16[2,1,2048,768]{2,3,1,0:T(8,128)(2,1)}, bf16[2,1,51...) while((s32[]{:T(128)}, ...), condition=%wide.region_4.5_spmd, body=%wide.region_1.4_spmd.sunk | while | flops 3310348288 | bytes 258694880 | solution.py:124
  258.6 32.2 %fusion.174 = (f32[12,512]{1,0:T(8,128)S(1)}, f32[12,512,2048]{2,1,0:T(8,128)}) fusion(f32[12,512,2048]{2,1,0:T(8,128)} %get-tuple-element.558, bf16[512,12,64]{0,2,1:T(8,128)(2,1)S(1)} %bitcast.265, bf16[2048,12,64]{0,2,1:T(8,128)(2,1)} %bitcast.257, pred[512,2048]{1,0:T(8,128)(4,1)S(1)} %broadcast_compare_fusion.4), kind=kOutput, calls=%fused_computation.202.clone.1 | convolution fusion | flops 1648355328 | bytes 105668608 | tf_op jit(solution)/shard_map/while/body/eval_jaxpr/rqhd,rkhd->rhqk/dot_general | solution.py:90
  340.1 32.2 %fusion.174 = (f32[12,512]{1,0:T(8,128)S(1)}, f32[12,512,2048]{2,1,0:T(8,128)}) fusion(f32[12,512,2048]{2,1,0:T(8,128)} %get-tuple-element.558, bf16[512,12,64]{0,2,1:T(8,128)(2,1)S(1)} %bitcast.265, bf16[2048,12,64]{0,2,1:T(8,128)(2,1)} %bitcast.257, pred[512,2048]{1,0:T(8,128)(4,1)S(1)} %broadcast_compare_fusion.4), kind=kOutput, calls=%fused_computation.202.clone.1 | convolution fusion | flops 1648355328 | bytes 105668608 | tf_op jit(solution)/shard_map/while/body/eval_jaxpr/rqhd,rkhd->rhqk/dot_general | solution.py:90
  432.2 31.0 %multiply_convert_fusion.1 = (bf16[2,512,3072]{2,1,0:T(8,128)(2,1)S(1)}, f32[2,512,3072]{2,1,0:T(8,128)}) fusion(f32[2,512,3072]{2,1,0:T(8,128)S(1)} %get-tuple-element.359, u8[512,3072]{1,0:T(8,128)(4,1)} %get-tuple-element.282, u8[512,3072]{1,0:T(8,128)(4,1)} %get-tuple-element.281), kind=kLoop, calls=%fused_computation.55 | loop fusion | flops 220200960 | bytes 34603008 | tf_op jit(solution)/shard_map/convert_element_type | solution.py:141
  481.8 31.1 %all_gather.18 = bf16[128,768]{1,0:T(8,128)(2,1)S(1)} all-gather(bf16[16,768]{1,0:T(8,128)(2,1)S(1)} %multiply_convert_fusion.6), channel_id=1, replica_groups=mesh['dp'=8,'seq'=4] {'dp'}, dimensions={0}, use_global_device_ids=true | all-gather | bytes 221184 | tf_op jit(solution)/shard_map/all_gather | solution.py:160
  515.3 59.0 %reduce-scatter.30.cloned.1.call-done = f32[16,768]{1,0:T(8,128)} async-done(((f32[128,768]{1,0:T(8,128)}), f32[16,768]{1,0:T(8,128)}) %reduce-scatter.30.cloned.1.call-update) | async-done | bytes 49168 | tf_op jit(solution)/shard_map/reduce_scatter | solution.py:183
  614.1 476.4 %while.30 = (s32[]{:T(128)}, bf16[2,1,512,768]{2,3,1,0:T(8,128)(2,1)}, f32[2,32,12]{1,2,0:T(8,128)}, bf16[2,1,2048,768]{2,3,1,0:T(8,128)(2,1)}, bf16[2,1,2048,76...) while((s32[]{:T(128)}, ...), condition=%wide.region_20.21_spmd.clone, body=%wide.region_18.20_spmd.clone.sunk | while | flops 9039767552 | bytes 632176896 | solution.py:251
  621.3 34.5 %subtract_exponential_fusion.2 = f32[12,512,2048]{2,1,0:T(8,128)} fusion(f32[12,512,2048]{2,1,0:T(8,128)} %get-tuple-element.599, f32[12,512]{1,0:T(8,128)S(1)} %dynamic-slice_bitcast_fusion.2, pred[512,2048]{1,0:T(8,128)(4,1)S(1)} %broadcast_compare_fusion.5, bf16[512,12,64]{0,2,1:T(8,128)(2,1)S(1)} %bitcast.261, bf16[2048,12,64]{0,2,1:T(8,128)(2,1)} %bitcast.252), kind=kOutput, calls=%fused_computation.21.clone.1 | convolution fusion | flops 1648361472 | bytes 105668608 | tf_op jit(solution)/shard_map/while/body/eval_jaxpr/rqhd,rkhd->rhqk/dot_general | solution.py:90
  663.3 33.0 %multiply_reduce_fusion.7 = (f32[12,512]{1,0:T(8,128)S(1)}, f32[12,512,2048]{2,1,0:T(8,128)}) fusion(f32[12,512,2048]{2,1,0:T(8,128)} %subtract_exponential_fusion.2, bf16[512,12,64]{0,2,1:T(8,128)(2,1)S(1)} %bitcast.259, bf16[2048,12,64]{0,2,1:T(8,128)(2,1)} %bitcast.256), kind=kOutput, calls=%fused_computation.20.clone.1 | convolution fusion | flops 1635772416 | bytes 104620032 | tf_op jit(solution)/shard_map/while/body/eval_jaxpr/rqhd,rkhd->rhqk/dot_general | solution.py:208
  696.3 40.1 %multiply_convert_fusion.11 = bf16[12,512,2048]{2,1,0:T(8,128)(2,1)} fusion(f32[12,512,2048]{2,1,0:T(8,128)} %subtract_exponential_fusion.2, f32[12,512,2048]{2,1,0:T(8,128)} %get-tuple-element.526, f32[12,512]{1,0:T(8,128)S(1)} %get-tuple-element.527), kind=kLoop, calls=%fused_computation.19.clone.1 | loop fusion | flops 37748736 | bytes 125853696 | tf_op jit(solution)/shard_map/while/body/eval_jaxpr/convert_element_type | solution.py:215
  771.4 44.5 %copy.136 = bf16[12,512,2048]{1,0,2:T(8,128)(2,1)} copy(bf16[12,512,2048]{2,1,0:T(8,128)(2,1)} %multiply_convert_fusion.11) | data formatting | bytes 50331648 | tf_op jit(solution)/shard_map/while/body/eval_jaxpr/convert_element_type | solution.py:215
  859.5 34.5 %subtract_exponential_fusion.2 = f32[12,512,2048]{2,1,0:T(8,128)} fusion(f32[12,512,2048]{2,1,0:T(8,128)} %get-tuple-element.599, f32[12,512]{1,0:T(8,128)S(1)} %dynamic-slice_bitcast_fusion.2, pred[512,2048]{1,0:T(8,128)(4,1)S(1)} %broadcast_compare_fusion.5, bf16[512,12,64]{0,2,1:T(8,128)(2,1)S(1)} %bitcast.261, bf16[2048,12,64]{0,2,1:T(8,128)(2,1)} %bitcast.252), kind=kOutput, calls=%fused_computation.21.clone.1 | convolution fusion | flops 1648361472 | bytes 105668608 | tf_op jit(solution)/shard_map/while/body/eval_jaxpr/rqhd,rkhd->rhqk/dot_general | solution.py:90
  901.4 32.6 %multiply_reduce_fusion.7 = (f32[12,512]{1,0:T(8,128)S(1)}, f32[12,512,2048]{2,1,0:T(8,128)}) fusion(f32[12,512,2048]{2,1,0:T(8,128)} %subtract_exponential_fusion.2, bf16[512,12,64]{0,2,1:T(8,128)(2,1)S(1)} %bitcast.259, bf16[2048,12,64]{0,2,1:T(8,128)(2,1)} %bitcast.256), kind=kOutput, calls=%fused_computation.20.clone.1 | convolution fusion | flops 1635772416 | bytes 104620032 | tf_op jit(solution)/shard_map/while/body/eval_jaxpr/rqhd,rkhd->rhqk/dot_general | solution.py:208
  934.0 40.0 %multiply_convert_fusion.11 = bf16[12,512,2048]{2,1,0:T(8,128)(2,1)} fusion(f32[12,512,2048]{2,1,0:T(8,128)} %subtract_exponential_fusion.2, f32[12,512,2048]{2,1,0:T(8,128)} %get-tuple-element.526, f32[12,512]{1,0:T(8,128)S(1)} %get-tuple-element.527), kind=kLoop, calls=%fused_computation.19.clone.1 | loop fusion | flops 37748736 | bytes 125853696 | tf_op jit(solution)/shard_map/while/body/eval_jaxpr/convert_element_type | solution.py:215
  1009.0 44.5 %copy.136 = bf16[12,512,2048]{1,0,2:T(8,128)(2,1)} copy(bf16[12,512,2048]{2,1,0:T(8,128)(2,1)} %multiply_convert_fusion.11) | data formatting | bytes 50331648 | tf_op jit(solution)/shard_map/while/body/eval_jaxpr/convert_element_type | solution.py:215
  1120.6 37.5 %reduce-scatter.36.cloned.1.call-done = bf16[96,768]{1,0:T(8,128)(2,1)} async-done(((bf16[768,768]{1,0:T(8,128)(2,1)}), bf16[96,768]{1,0:T(8,128)(2,1)}) %reduce-scatter.36.cloned.1.call-update) | async-done | bytes 147472 | tf_op jit(solution)/shard_map/reduce_scatter | solution.py:281
  1160.0 96.1 %reduce-scatter.48.cloned.1.call-done = bf16[384,768]{1,0:T(8,128)(2,1)} async-done(((bf16[3072,768]{1,0:T(8,128)(2,1)}), bf16[384,768]{1,0:T(8,128)(2,1)}) %reduce-scatter.48.cloned.1.call-update) | async-done | bytes 589840 | tf_op jit(solution)/shard_map/reduce_scatter | solution.py:296
  1258.3 96.6 %reduce-scatter.44.cloned.1.call-done = bf16[96,3072]{1,0:T(8,128)(2,1)} async-done(((bf16[768,3072]{1,0:T(8,128)(2,1)}), bf16[96,3072]{1,0:T(8,128)(2,1)}) %reduce-scatter.44.cloned.1.call-update) | async-done | bytes 589840 | tf_op jit(solution)/shard_map/reduce_scatter | solution.py:293
  1355.0 60.6 %reduce-scatter.32.cloned.1.call-done = bf16[2,512,768]{1,2,0:T(8,128)(2,1)} async-done(((bf16[2,2048,768]{1,2,0:T(8,128)(2,1)}), bf16[2,512,768]{1,2,0:T(8,128)(2,1)}) %reduce-scatter.32.cloned.1.call-update) | async-done | bytes 1572880 | tf_op jit(solution)/shard_map/reduce_scatter | solution.py:253
  1419.8 56.8 %reduce-scatter.34.cloned.1.call-done = bf16[2,512,768]{1,2,0:T(8,128)(2,1)} async-done(((bf16[2,2048,768]{1,2,0:T(8,128)(2,1)}), bf16[2,512,768]{1,2,0:T(8,128)(2,1)}) %reduce-scatter.34.cloned.1.call-update) | async-done | bytes 1572880 | tf_op jit(solution)/shard_map/reduce_scatter | solution.py:259
  1599.6 60.9 %reduce-scatter.38.cloned.1.call-done = bf16[96,768]{1,0:T(8,128)(2,1)} async-done(((bf16[768,768]{1,0:T(8,128)(2,1)}), bf16[96,768]{1,0:T(8,128)(2,1)}) %reduce-scatter.38.cloned.1.call-update) | async-done | bytes 147472 | tf_op jit(solution)/shard_map/reduce_scatter | solution.py:284
  1669.4 40.5 %all-reduce = (f32[]{:T(128)}, f32[768]{0:T(1024)}, f32[768]{0:T(1024)}, f32[32,12]{0,1:T(8,128)}) all-reduce(f32[]{:T(128)S(6)} %div.78, f32[768]{0:T(1024)S(1)} %get-tuple-element.285, f32[768]{0:T(1024)S(1)} %copy-done.40, f32[32,12]{0,1:T(8,128)S(1)} %reduce_sum.171), channel_id=1, replica_groups=mesh['dp'=8,'seq'=4] {'dp','seq'}, use_global_device_ids=true, to_apply=%region_14.15 | all-reduce | flops 1921 | bytes 15368 | tf_op jit(solution)/shard_map/psum | solution.py:326
  (301 shorter events, 711.7 us)
Async XLA Ops:
  7.2 223.7 %all-gather.4.cloned.1.call-start = ((), (), s32[]{:S(2)}) async-start(), calls=%async_computation.17 | async-start | bytes 7864320 | tf_op jit(solution)/shard_map/all_gather | solution.py:121
  13.9 225.8 %all-gather.6.cloned.1.call-start = ((), (), s32[]{:S(2)}) async-start(), calls=%async_computation.18 | async-start | bytes 7864320 | tf_op jit(solution)/shard_map/all_gather | solution.py:120
  17.9 556.5 %reduce-scatter.30.cloned.1.call-start = ((), (), s32[]{:S(2)}) async-start(), calls=%async_computation.19 | async-start | bytes 442368 | tf_op jit(solution)/shard_map/reduce_scatter | solution.py:183
  418.1 188.2 %copy-start.32 = (f32[2,512]{1,0:T(2,128)}, f32[2,512]{1,0:T(2,128)S(1)}, u32[]{:S(2)}) copy-start(f32[2,512]{1,0:T(2,128)S(1)} %fusion.103) | copy-start | bytes 12292
  515.2 601.7 %reduce-scatter.50.cloned.1.call-start = ((), (), s32[]{:S(2)}) async-start(), calls=%async_computation.29 | async-start | bytes 1327104 | tf_op jit(solution)/shard_map/reduce_scatter | solution.py:299
  577.6 541.2 %reduce-scatter.42.cloned.1.call-start = ((), (), s32[]{:S(2)}) async-start(), calls=%async_computation.25 | async-start | bytes 1327104 | tf_op jit(solution)/shard_map/reduce_scatter | solution.py:290
  612.7 545.5 %reduce-scatter.36.cloned.1.call-start = ((), (), s32[]{:S(2)}) async-start(), calls=%async_computation.22 | async-start | bytes 1327104 | tf_op jit(solution)/shard_map/reduce_scatter | solution.py:281
  614.1 476.4 %copy-start.26 = (f32[2,512]{1,0:T(2,128)S(1)}, f32[2,512]{1,0:T(2,128)}, u32[]{:S(2)}) copy-start(f32[2,512]{1,0:T(2,128)} %copy-done.24) | copy-start | bytes 12292
  614.1 476.4 %copy-start.29 = (f32[768]{0:T(1024)S(1)}, f32[768]{0:T(1024)}, u32[]{:S(2)}) copy-start(f32[768]{0:T(1024)} %param.27) | copy-start | bytes 9220
  1095.1 161.0 %reduce-scatter.48.cloned.1.call-start = ((), (), s32[]{:S(2)}) async-start(), calls=%async_computation.28 | async-start | bytes 5308416 | tf_op jit(solution)/shard_map/reduce_scatter | solution.py:296
  1104.8 250.1 %reduce-scatter.44.cloned.1.call-start = ((), (), s32[]{:S(2)}) async-start(), calls=%async_computation.26 | async-start | bytes 5308416 | tf_op jit(solution)/shard_map/reduce_scatter | solution.py:293
  1115.5 300.1 %reduce-scatter.32.cloned.1.call-start = ((), (), s32[]{:S(2)}) async-start(), calls=%async_computation.20 | async-start | bytes 7864320 | tf_op jit(solution)/shard_map/reduce_scatter | solution.py:253
  1116.2 360.3 %reduce-scatter.34.cloned.1.call-start = ((), (), s32[]{:S(2)}) async-start(), calls=%async_computation.21 | async-start | bytes 7864320 | tf_op jit(solution)/shard_map/reduce_scatter | solution.py:259
  1116.8 298.8 %copy-start.7 = (bf16[2,512,768]{2,1,0:T(8,128)(2,1)S(1)}, bf16[2,512,768]{2,1,0:T(8,128)(2,1)}, u32[]{:S(2)}) copy-start(bf16[2,512,768]{2,1,0:T(8,128)(2,1)} %param.17) | copy-start | bytes 4718596
  1116.8 381.9 %reduce-scatter.62.cloned.1.call-start = ((), (), s32[]{:S(2)}) async-start(), calls=%async_computation.35 | async-start | bytes 245760
  1118.8 402.7 %reduce-scatter.58.cloned.1.call-start = ((), (), s32[]{:S(2)}) async-start(), calls=%async_computation.33 | async-start | bytes 245760
  1120.6 423.6 %reduce-scatter.52.cloned.1.call-start = ((), (), s32[]{:S(2)}) async-start(), calls=%async_computation.30 | async-start | bytes 245760
  1159.9 408.7 %reduce-scatter.60.cloned.1.call-start = ((), (), s32[]{:S(2)}) async-start(), calls=%async_computation.34 | async-start | bytes 737280
  1258.2 334.9 %reduce-scatter.46.cloned.1.call-start = ((), (), s32[]{:S(2)}) async-start(), calls=%async_computation.27 | async-start | bytes 737280 | tf_op jit(solution)/shard_map/reduce_scatter | solution.py:316
  1354.9 305.5 %reduce-scatter.38.cloned.1.call-start = ((), (), s32[]{:S(2)}) async-start(), calls=%async_computation.23 | async-start | bytes 1327104 | tf_op jit(solution)/shard_map/reduce_scatter | solution.py:284
  1419.7 307.2 %reduce-scatter.40.cloned.1.call-start = ((), (), s32[]{:S(2)}) async-start(), calls=%async_computation.24 | async-start | bytes 1327104 | tf_op jit(solution)/shard_map/reduce_scatter | solution.py:287
  1480.6 267.4 %reduce-scatter.54.cloned.1.call-start = ((), (), s32[]{:S(2)}) async-start(), calls=%async_computation.31 | async-start | bytes 245760
  1662.2 48.4 %copy-start.31 = (f32[2,512]{1,0:T(2,128)S(1)}, f32[2,512]{1,0:T(2,128)}, u32[]{:S(2)}) copy-start(f32[2,512]{1,0:T(2,128)} %copy-done.30) | copy-start | bytes 12292
  1662.2 108.0 %reduce-scatter.56.cloned.1.call-start = ((), (), s32[]{:S(2)}) async-start(), calls=%async_computation.32 | async-start | bytes 245760
  (51 other events, 749.7 us)
Sparse Core Ops, SparseCore 0:
  14.0 49.0 all-gather.3
  65.3 46.3 all-gather.5
  515.4 58.9 reduce-scatter.29
  577.8 63.0 reduce-scatter.49
  644.1 62.9 reduce-scatter.41
  1095.2 62.9 reduce-scatter.35
  1161.8 94.2 reduce-scatter.47
  1259.7 95.1 reduce-scatter.43
  1357.5 58.0 reduce-scatter.31
  1418.1 58.3 reduce-scatter.33
  1479.0 19.7 reduce-scatter.61
  1501.6 19.7 reduce-scatter.57
  1524.4 19.7 reduce-scatter.51
  1546.6 22.0 reduce-scatter.59
  1571.0 22.0 reduce-scatter.45
  1596.3 64.0 reduce-scatter.37
  1663.7 63.2 reduce-scatter.39
  1729.2 18.7 reduce-scatter.53
  1750.5 19.7 reduce-scatter.55
where the time goes:
time: 1790 us; the launch traced here: 1780 us
  waiting for transfers between devices  620 us (35%)
  matrix products  613 us (34%)
  local copies, waits for them, and re-layouts  241 us (13%)
  other arithmetic  177 us (10%)
  blocking collectives  109 us (6%)
    dot_general x4, matrix products, masked_scores(): jnp.einsum('rqhd,rkhd->rhqk', by_heads(query_block), by_heads(key_block),...  133 us
    unnamed x25, waiting for transfers between devices  113 us
    reduce_scatter x1, waiting for transfers between devices, on_device(): lax.psum_scatter(grad_wup.astype(jnp.bfloat16), 'dp', scatter_dimension=0...  96.6 us
    reduce_scatter x1, waiting for transfers between devices, on_device(): lax.psum_scatter(grad_wdown.astype(jnp.bfloat16), 'dp', scatter_dimension...  96.1 us
    convert_element_type x2, local copies, waits for them, and re-layouts, query_side(): grad_scores = (weights * (grad_weights - centre)).astype(jnp.bfloat16)  89.1 us
    convert_element_type x2, other arithmetic, query_side(): grad_scores = (weights * (grad_weights - centre)).astype(jnp.bfloat16)  80 us
    dot_general x1, matrix products, bias_from(): jnp.einsum('qkb,bh->hqk', onehot, high_part, preferred_element_type=jnp.f...  67.2 us
    dot_general x2, matrix products, query_side(): jnp.einsum('rqhd,rkhd->rhqk', by_heads(grad_block_in), by_heads(value_blo...  65.6 us
  transfers between devices with their start and end apart: 19, of which 15 were waited for; matrix products, arithmetic and copies ran while one was open for 44% of the time, Pallas kernels for 0%

commit v1 on v0

v1 whole, which is shorter than its diff:
```python
import functools

import jax
import jax.numpy as jnp
from jax import lax
from jax.experimental import pallas as pl
from jax.experimental.pallas import tpu as pltpu
from jax.sharding import PartitionSpec as P

EPS = 1e-06
LOGIT_SCALE = 20.0
LIMITS = (12, 16, 23, 32, 46, 64, 91)
MASKED = -float(2**30)
TILE = 256
SPAN = 1024
BLOCK = 128
BANDS = 5
F32 = jnp.float32
BF16 = jnp.bfloat16
MIB = 1024 * 1024


def bucket_of(offset, half_count):
    distance = jnp.abs(offset)
    beyond = 8 + sum(((distance >= bound_at).astype(jnp.int32) for bound_at in LIMITS))
    nearby = jnp.where(distance < 8, distance, beyond)
    return nearby + half_count * (offset > 0).astype(jnp.int32)


def diagonal_offsets():
    diff = (jnp.arange(BANDS, dtype=jnp.int32) - BANDS // 2)[:, None] * BLOCK
    place = jnp.arange(2 * BLOCK, dtype=jnp.int32)[None, :]
    return diff - jnp.where(place < BLOCK, place, place - 2 * BLOCK)


def dot(left, right):
    return jnp.dot(left, right, preferred_element_type=F32)


def dot_nt(left, right):
    return lax.dot_general(left, right, (((1,), (1,)), ((), ())), preferred_element_type=F32)


def three_parts(value):
    high = value.astype(BF16).astype(F32)
    rest = value - high
    middle = rest.astype(BF16).astype(F32)
    return high, middle, rest - middle


def toeplitz(vector):
    rows, size = vector, 1
    while size < BLOCK:
        rows = jnp.concatenate([rows, pltpu.roll(rows, size, 1)], axis=0)
        size *= 2
    return rows[:, :BLOCK]


def diagonal_sums(block):
    rows, size = jnp.concatenate([block, jnp.zeros_like(block)], axis=1), BLOCK
    while size > 1:
        size //= 2
        rows = rows[:size] + pltpu.roll(rows[size:], 2 * BLOCK - size, 1)
    return rows


def blocks_of(band):
    for key in range(TILE // BLOCK):
        for query in range(TILE // BLOCK):
            apart = (band - BANDS // 2) * (TILE // BLOCK) + key - query
            row = min(max(apart, -(BANDS // 2)), BANDS // 2) + BANDS // 2
            yield pl.ds(key * BLOCK, BLOCK), pl.ds(query * BLOCK, BLOCK), row


def bias_tiles(diag_ref, bias):
    rows = [diag_ref[0, row : row + 1, :] for row in range(BANDS)]
    blocks = [toeplitz(row) for row in rows[1:-1]]
    blocks = [jnp.broadcast_to(rows[0][:, :BLOCK], (BLOCK, BLOCK))] + blocks
    blocks += [jnp.broadcast_to(rows[-1][:, :BLOCK], (BLOCK, BLOCK))]
    for band in range(BANDS):
        for keys, queries, row in blocks_of(band):
            bias[band, keys, queries] = blocks[row]


def segment_rows(seg, slots, inside, outside):
    iota = lax.broadcasted_iota(jnp.int32, (slots, seg.shape[1]), 0)
    return jnp.where(iota == seg, inside, outside).astype(F32)


def extended(head, seg_part, stat_rows):
    width = head.shape[1]
    stat = jnp.concatenate(
        list(stat_rows) + [jnp.zeros((8 - len(stat_rows), width), F32)], axis=0
    )
    more = jnp.concatenate([seg_part, stat], axis=0).astype(BF16)
    rest = jnp.zeros((128 - head.shape[0] - more.shape[0], width), BF16)
    return jnp.concatenate([head, more, rest], axis=0)


def keys_side(source_ref, seg_ref, target_ref, slots):
    length = source_ref.shape[3]
    for at in range(0, length, TILE):
        part = pl.ds(at, TILE)
        seg_part = segment_rows(seg_ref[0:1, part], slots, 1.0, 0.0)
        one = jnp.ones((1, TILE), F32)
        whole = extended(source_ref[0, 0, :, part], seg_part, [one, one, one])
        whole = jnp.transpose(whole.astype(F32)).astype(BF16)
        target_ref[part, :] = whole
        target_ref[pl.ds(length + at, TILE), :] = whole


def band_of(chunk, tile):
    return jnp.clip(chunk - tile, -(BANDS // 2), BANDS // 2) + BANDS // 2


def tile_part(tile):
    return pl.ds(pl.multiple_of(tile * TILE, TILE), TILE)


def chunk_at(tile, turn, count):
    return lax.rem(tile + turn, count)


def span_part(span, tile):
    return pl.ds(pl.multiple_of(tile * TILE, TILE) + span * SPAN, SPAN)


def is_far(turn, count):
    return 2 <= turn <= count - 2


def forward_kernel(
    slots, q_ref, k_ref, v_ref, seg_ref, diag_ref, o_ref, ob_ref, inv_ref, p_ref, kx, bias, held
):
    count, spans = k_ref.shape[3] // TILE, k_ref.shape[3] // SPAN
    keys_side(k_ref, seg_ref, kx, slots)
    bias_tiles(diag_ref, bias)
    before, after = diag_ref[0, 0:1, 0:1], diag_ref[0, BANDS - 1 : BANDS, 0:1]

    def query_side(tile):
        part = tile_part(tile)
        return extended(q_ref[0, 0, :, part], segment_rows(seg_ref[0:1, part], slots, 0.0, MASKED), [])

    def score(span, tile, qx, top):
        products = dot(kx[span_part(span, tile), :], qx)
        for sub in range(SPAN // TILE):
            turn = span * (SPAN // TILE) + sub
            chunk = chunk_at(tile, turn, count)
            if is_far(turn, count):
                added = jnp.where(chunk > tile, after, before)
            else:
                added = bias[band_of(chunk, tile)]
            scores = products[sub * TILE : (sub + 1) * TILE] + added
            held[turn] = scores
            top = jnp.maximum(top, jnp.max(scores.reshape(TILE // 8, 8, TILE), axis=0))
        return top

    def weigh(turn, tile, top, total, out):
        chunk = tile_part(chunk_at(tile, turn, count))
        weights = jnp.exp(held[turn] - top)
        total = total + jnp.sum(weights.reshape(TILE // 8, 8, TILE), axis=0)
        weights = weights.astype(BF16)
        p_ref[0, chunk, tile_part(tile)] = weights
        return total, out + dot(v_ref[0, 0, :, chunk], weights)

    def finish(tile, total, out):
        part = tile_part(tile)
        inverse = 1.0 / jnp.sum(total, axis=0, keepdims=True)
        out = out * inverse
        o_ref[0, :, part] = out
        ob_ref[0, :, part] = out.astype(BF16)
        inv_ref[0, :, part] = inverse

    lowest = jnp.full((8, TILE), -jnp.inf, F32)
    start = (jnp.zeros((8, TILE), F32), jnp.zeros((v_ref.shape[2], TILE), F32))

    def body(tile, top):
        qx, following = query_side(tile + 1), lowest
        total, out = start
        for span in range(spans):
            for turn in range(span * (SPAN // TILE), (span + 1) * (SPAN // TILE)):
                total, out = weigh(turn, tile, top, total, out)
            following = score(span, tile + 1, qx, following)
        finish(tile, total, out)
        return jnp.max(following, axis=0, keepdims=True)

    qx, top = query_side(0), lowest
    for span in range(spans):
        top = score(span, 0, qx, top)
    top = lax.fori_loop(0, count - 1, body, jnp.max(top, axis=0, keepdims=True))
    total, out = start
    for turn in range(count):
        total, out = weigh(turn, count - 1, top, total, out)
    finish(count - 1, total, out)


def head_spec(rows, length):
    return pl.BlockSpec((1, rows, length), lambda h: (h, 0, 0))


def part_spec(part, width, length):
    return pl.BlockSpec((1, 1, width, length), lambda h: (h, part, 0, 0))


def attention_forward(slots, qkv, seg_row, diag):
    heads, _, width, length = qkv.shape
    return pl.pallas_call(
        functools.partial(forward_kernel, slots),
        grid=(heads,),
        in_specs=[part_spec(part, width, length) for part in range(3)]
        + [pl.BlockSpec(seg_row.shape, lambda h: (0, 0)), head_spec(8, 2 * BLOCK)],
        out_specs=[
            head_spec(width, length),
            head_spec(width, length),
            head_spec(1, length),
            head_spec(length, length),
        ],
        out_shape=[
            jax.ShapeDtypeStruct((heads, width, length), F32),
            jax.ShapeDtypeStruct((heads, width, length), BF16),
            jax.ShapeDtypeStruct((heads, 1, length), F32),
            jax.ShapeDtypeStruct((heads, length, length), BF16),
        ],
        scratch_shapes=[
            pltpu.VMEM((2 * length, 128), BF16),
            pltpu.VMEM((BANDS, TILE, TILE), F32),
            pltpu.VMEM((length // TILE, TILE, TILE), F32),
        ],
        compiler_params=pltpu.CompilerParams(
            dimension_semantics=("arbitrary",), vmem_limit_bytes=56 * MIB
        ),
        cost_estimate=pl.CostEstimate(
            flops=heads * length * length * 512,
            bytes_accessed=heads * length * (width * 12 + length * 2),
            transcendentals=heads * length * length,
        ),
        name="attention_forward",
    )(qkv, qkv, qkv, seg_row, diag)


def remote(source, target, send, receive, where):
    return pltpu.make_async_remote_copy(
        src_ref=source,
        dst_ref=target,
        send_sem=send,
        recv_sem=receive,
        device_id=where,
        device_id_type=pl.DeviceIdType.MESH,
    )


def signal(barrier, where):
    pl.semaphore_signal(barrier, inc=1, device_id=where, device_id_type=pl.DeviceIdType.MESH)


def each(first, last, step):
    def body(index, carried):
        step(index)
        return carried

    lax.fori_loop(first, last, body, 0)


def head_backward(
    q_ref,
    k_ref,
    v_ref,
    g_ref,
    o_ref,
    inv_ref,
    p_ref,
    d_ref,
    dd_ref,
    vx,
    sums,
    far,
    dkv,
    gx,
    both,
    weighed,
    left,
    beside=None,
):
    width, length = k_ref.shape[2], k_ref.shape[3]
    count, subs = length // TILE, SPAN // TILE
    for at in range(0, length, TILE):
        part = pl.ds(at, TILE)
        ones = jnp.ones((8, TILE), BF16)
        rest = jnp.zeros((128 - width - 8, TILE), BF16)
        whole = jnp.concatenate([v_ref[0, 0, :, part], ones, rest], axis=0)
        whole = jnp.transpose(whole.astype(F32)).astype(BF16)
        vx[part, :] = whole
        vx[pl.ds(length + at, TILE), :] = whole
    sums[...] = jnp.zeros_like(sums)
    far[...] = jnp.zeros_like(far)
    dkv[...] = jnp.zeros_like(dkv)
    both[1] = jnp.zeros_like(both[1])
    left[1] = jnp.zeros_like(left[1])

    def queries_side(tile, slot):
        own = tile_part(tile)
        query, grad = q_ref[0, 0, :, own], g_ref[0, :, own].astype(F32)
        inverse = inv_ref[0, :, own]
        centre = jnp.sum(grad * o_ref[0, :, own], axis=0, keepdims=True) * inverse
        grad = (grad * inverse).astype(BF16)
        stats = jnp.concatenate(list(three_parts(-centre)) + [jnp.zeros((5, TILE), F32)], axis=0)
        gx[slot] = jnp.concatenate(
            [grad, stats.astype(BF16), jnp.zeros((128 - width - 8, TILE), BF16)], axis=0
        )
        nothing = jnp.zeros((width, TILE), F32)
        upper = jnp.transpose(jnp.concatenate([query.astype(F32), nothing], axis=0))
        lower = jnp.transpose(jnp.concatenate([nothing, grad.astype(F32)], axis=0))
        both[slot] = jnp.concatenate([upper, lower], axis=0).astype(BF16)

    def weigh(tile, span, slot):
        weighed[span] = dot(vx[span_part(span, tile), :], gx[slot])

    def score(tile, span):
        for sub in range(subs):
            turn, rows = span * subs + sub, pl.ds(sub * TILE, TILE)
            chunk = chunk_at(tile, turn, count)
            weights = p_ref[0, tile_part(chunk), tile_part(tile)]
            grad_scores = weights.astype(F32) * weighed[span, rows, :]
            if is_far(turn, count):
                side = (chunk > tile).astype(jnp.int32)
                far[side] += jnp.sum(grad_scores.reshape(TILE // 8, 8, TILE), axis=0)
            else:
                sums[band_of(chunk, tile)] += grad_scores
            left[span, rows, :TILE] = grad_scores.astype(BF16)
            left[span, rows, TILE:] = weights

    def gather(tile, span, slot, grad_query):
        products = dot(left[span], both[slot])
        for sub in range(subs):
            part = tile_part(chunk_at(tile, span * subs + sub, count))
            rows = slice(sub * TILE, (sub + 1) * TILE)
            dkv[part, :] += products[rows]
            grad_query = grad_query + dot(k_ref[0, 0, :, part], left[span, rows, :TILE])
        return grad_query

    def store(tile, grad_query):
        d_ref[0, 0, :, tile_part(tile)] = grad_query.astype(BF16)

    empty = jnp.zeros((width, TILE), F32)

    def step(tile, slot, following, behind, grad_behind):
        weigh(tile, 1, slot)
        score(tile, 0)
        store(behind, gather(behind, 1, 1 - slot, grad_behind))
        queries_side(following, 1 - slot)
        weigh(following, 0, 1 - slot)
        score(tile, 1)
        return gather(tile, 0, slot, empty)

    def one(tile, carried):
        if beside is not None:
            beside(tile)
        slot = lax.rem(tile, 2)
        return step(tile, slot, lax.rem(tile + 1, count), lax.rem(tile + count - 1, count), carried)

    queries_side(0, 0)
    weigh(0, 0, 0)
    carried = lax.fori_loop(0, count, one, empty)
    store(count - 1, gather(count - 1, 1, 1, carried))
    d_both = jnp.transpose(dkv[...])
    d_ref[0, 1] = d_both[:width].astype(BF16)
    d_ref[0, 2] = d_both[width:].astype(BF16)
    totals = [None] * BANDS
    for band in range(BANDS):
        for keys, queries, row in blocks_of(band):
            block = sums[band, keys, queries]
            if row in (0, BANDS - 1):
                block = jnp.sum(block.reshape(BLOCK // 8, 8, BLOCK), axis=0)
            totals[row] = block if totals[row] is None else totals[row] + block
    for row, total in enumerate(totals):
        if row in (0, BANDS - 1):
            more = far[min(row, 1)]
            total = jnp.sum(total + more[:, :BLOCK] + more[:, BLOCK:], axis=0, keepdims=True)
            total = jnp.concatenate([total, jnp.zeros_like(total)], axis=1)
        else:
            total = diagonal_sums(total)
        dd_ref[0, row : row + 1, :] = total
    dd_ref[0, BANDS:, :] = jnp.zeros((8 - BANDS, 2 * BLOCK), F32)


def added(left, right):
    return (left.astype(F32) + right.astype(F32)).astype(BF16)


def backward_kernel(
    dp_size,
    q_ref,
    k_ref,
    v_ref,
    g_ref,
    o_ref,
    inv_ref,
    p_ref,
    normed_ref,
    up_ref,
    out_ref,
    d_ref,
    dd_ref,
    g_up_ref,
    g_out_ref,
    g_late_ref,
    last_ref,
    vx,
    sums,
    far,
    dkv,
    gx,
    both,
    weighed,
    left,
    up_near,
    out_near,
    up_far,
    out_far,
    late_out,
    late_near,
    late_total,
    late_far,
    chip_send,
    chip_recv,
    late_send,
    late_recv,
    dp_send,
    dp_recv,
):
    head, heads = pl.program_id(0), pl.num_programs(0)
    own_heads = late_near.shape[0]
    dp_at, seq_at = lax.axis_index("dp"), lax.axis_index("seq")
    chip = seq_at // 2
    rows = g_up_ref.shape[0]
    other_chip = {"dp": dp_at, "seq": lax.rem(seq_at + 2, 4)}
    peer = lambda step: {"dp": lax.rem(dp_at + step, dp_size), "seq": seq_at}
    source_of = lambda step: lax.rem(dp_at + step, dp_size)
    rows_of = lambda which: pl.ds(pl.multiple_of(which * rows, rows), rows)

    def chip_copies():
        side, there = [up_ref.at[1 - chip], out_ref.at[1 - chip]], [up_near, out_near]
        return [
            remote(source, target, chip_send.at[at], chip_recv.at[at], other_chip)
            for at, (source, target) in enumerate(zip(side, there))
        ]

    def dp_copy(kind, step, source):
        to = rows_of(lax.rem(dp_at + step, dp_size))
        if kind == 0:
            item, there = up_near.at[to, :], up_far.at[source]
        elif kind == 1:
            item, there = out_near.at[to, :], out_far.at[source]
        else:
            item, there = late_total.at[kind - 2, to, :], late_far.at[kind - 2, source]
        return remote(item, there, dp_send.at[kind, step], dp_recv.at[kind, source], peer(step))

    def late_copy(which):
        return remote(
            late_out.at[which], late_near.at[which], late_send.at[which], late_recv.at[which], other_chip
        )

    @pl.when(head == 0)
    def _():
        barrier = pltpu.get_barrier_semaphore()
        signal(barrier, other_chip)
        each(1, dp_size, lambda step: signal(barrier, peer(step)))
        pl.semaphore_wait(barrier, dp_size)
        for copy in chip_copies():
            copy.start()

    def beside(index):
        @pl.when((head == own_heads - 1) & (index == 2))
        def _():
            for copy in chip_copies():
                copy.wait_recv()

            def body(block):
                part = rows_of(block)
                up_near[part, :] = added(up_ref[chip, part, :], up_near[part, :])
                out_near[part, :] = added(out_ref[chip, part, :], out_near[part, :])

            each(0, dp_size, body)
            for kind in range(2):
                each(1, dp_size, lambda step: dp_copy(kind, step, dp_at).start())

    head_backward(
        q_ref,
        k_ref,
        v_ref,
        g_ref,
        o_ref,
        inv_ref,
        p_ref,
        d_ref,
        dd_ref,
        vx,
        sums,
        far,
        dkv,
        gx,
        both,
        weighed,
        left,
        beside,
    )
    grad_w = dot_nt(normed_ref[...], d_ref[0].reshape(-1, d_ref.shape[3]))

    @pl.when(head < own_heads)
    def _():
        late_out[head] = grad_w.astype(BF16)
        late_copy(head).start()

    for which in range(own_heads):

        @pl.when(head == own_heads + which)
        def _():
            late_copy(which).wait_recv()
            both = (grad_w + late_near[which].astype(F32)).astype(BF16)
            if which == own_heads - 1:
                last_ref[...] = both
            else:
                late_total[which] = both
                each(1, dp_size, lambda step: dp_copy(2 + which, step, dp_at).start())

    @pl.when(head == heads - 1)
    def _():
        for copy in chip_copies() + [late_copy(which) for which in range(own_heads)]:
            copy.wait_send()
        mine = rows_of(dp_at)
        totals = [
            up_near[mine, :].astype(F32),
            out_near[mine, :].astype(F32),
        ] + [late_total[which, mine, :].astype(F32) for which in range(own_heads - 1)]
        boxes = [up_far, out_far] + [late_far.at[which] for which in range(own_heads - 1)]
        for kind, box in enumerate(boxes):
            each(1, dp_size, lambda step: dp_copy(kind, step, source_of(step)).wait_recv())
            box[dp_at] = jnp.zeros(box.shape[1:], BF16)
            for source in range(dp_size):
                totals[kind] = totals[kind] + box[source].astype(F32)
            each(1, dp_size, lambda step: dp_copy(kind, step, dp_at).wait_send())
        g_up_ref[...] = totals[0]
        g_out_ref[...] = totals[1]
        for which in range(own_heads - 1):
            g_late_ref[which] = totals[2 + which]


def backward_specs(heads, width, length):
    specs = dict(
        in_specs=[part_spec(part, width, length) for part in range(3)]
        + [
            head_spec(width, length),
            head_spec(width, length),
            head_spec(1, length),
            head_spec(length, length),
        ],
        out_specs=[
            pl.BlockSpec((1, 3, width, length), lambda h: (h, 0, 0, 0)),
            head_spec(8, 2 * BLOCK),
        ],
        out_shape=[
            jax.ShapeDtypeStruct((heads, 3, width, length), BF16),
            jax.ShapeDtypeStruct((heads, 8, 2 * BLOCK), F32),
        ],
        scratch_shapes=[
            pltpu.VMEM((2 * length, 128), BF16),
            pltpu.VMEM((BANDS, TILE, TILE), F32),
            pltpu.VMEM((2, 8, TILE), F32),
            pltpu.VMEM((length, 128), F32),
            pltpu.VMEM((2, 128, TILE), BF16),
            pltpu.VMEM((2, 2 * TILE, 128), BF16),
            pltpu.VMEM((2, SPAN, TILE), F32),
            pltpu.VMEM((2, SPAN, 2 * TILE), BF16),
        ],
    )
    cost = pl.CostEstimate(
        flops=heads * length * length * 1024,
        bytes_accessed=heads * length * (width * 20 + length * 2),
        transcendentals=0,
    )
    return specs, cost


def attention_backward(qkv, g_t, o_t, inverse, probs):
    heads, _, width, length = qkv.shape
    specs, cost = backward_specs(heads, width, length)
    return pl.pallas_call(
        head_backward,
        grid=(heads,),
        compiler_params=pltpu.CompilerParams(
            dimension_semantics=("arbitrary",), vmem_limit_bytes=56 * MIB
        ),
        cost_estimate=cost,
        name="attention_backward",
        **specs,
    )(qkv, qkv, qkv, g_t, o_t, inverse, probs)


def attention_backward_and_sums(
    qkv, g_t, o_t, inverse, probs, normed_t, up_sum, out_sum, dp_size
):
    heads, _, width, length = qkv.shape
    specs, cost = backward_specs(heads, width, length)
    own_heads = heads // 2
    _, model, cols = up_sum.shape
    out_cols = out_sum.shape[2]
    rows, late = model // dp_size, 3 * width
    vmem = pl.BlockSpec(memory_space=pltpu.VMEM)
    dma = pltpu.SemaphoreType.DMA
    specs["in_specs"] += [vmem] * 3
    specs["out_specs"] += [vmem] * 4
    specs["out_shape"] += [
        jax.ShapeDtypeStruct((rows, cols), F32),
        jax.ShapeDtypeStruct((rows, out_cols), F32),
        jax.ShapeDtypeStruct((own_heads - 1, rows, late), F32),
        jax.ShapeDtypeStruct((model, late), BF16),
    ]
    specs["scratch_shapes"] += [
        pltpu.VMEM((model, cols), BF16),
        pltpu.VMEM((model, out_cols), BF16),
        pltpu.VMEM((dp_size, rows, cols), BF16),
        pltpu.VMEM((dp_size, rows, out_cols), BF16),
        pltpu.VMEM((own_heads, model, late), BF16),
        pltpu.VMEM((own_heads, model, late), BF16),
        pltpu.VMEM((own_heads - 1, model, late), BF16),
        pltpu.VMEM((own_heads - 1, dp_size, rows, late), BF16),
        dma((2,)),
        dma((2,)),
        dma((own_heads,)),
        dma((own_heads,)),
        dma((1 + own_heads, dp_size)),
        dma((1 + own_heads, dp_size)),
    ]
    return pl.pallas_call(
        functools.partial(backward_kernel, dp_size),
        grid=(heads,),
        compiler_params=pltpu.CompilerParams(
            dimension_semantics=("arbitrary",),
            vmem_limit_bytes=60 * MIB,
            collective_id=2,
            has_side_effects=True,
        ),
        cost_estimate=cost,
        name="attention_backward_and_sums",
        **specs,
    )(qkv, qkv, qkv, g_t, o_t, inverse, probs, normed_t, up_sum, out_sum)


def loss_terms(inbox, w_ref, slots, loss_ref, pooled_ref, grad_proj_ref, grad_block_ref):
    groups, _, lanes = inbox.shape
    model = 2 * (lanes - 128)
    every = inbox[...].astype(F32)
    many = groups * slots
    flat = lambda value: value.reshape(many, value.shape[2])
    pooled = jnp.concatenate(
        [flat(every[:, :slots, : model // 2]), flat(every[:, slots:, : model // 2])], axis=1
    ).astype(BF16)
    info = flat(every[:, :slots, model // 2 :])
    counts = info[:, 0:1] * 64.0 + info[:, 1:2]
    proj = dot(pooled, w_ref[...])
    inverse = lax.rsqrt(jnp.sum(proj * proj, axis=-1, keepdims=True) + EPS)
    embed = (proj * inverse).astype(BF16)
    logits = LOGIT_SCALE * dot_nt(embed, embed)
    rows_at = lax.broadcasted_iota(jnp.int32, (many, many), 0)
    self_mask = rows_at == lax.broadcasted_iota(jnp.int32, (many, many), 1)
    pairs = jnp.broadcast_to(info[:, 2:3], (many, many))
    partner = jnp.where(self_mask, 0.0, jnp.where(pairs == jnp.transpose(pairs), 1.0, 0.0))
    masked = jnp.where(self_mask, -1000000000.0, logits)
    top = jnp.max(masked, axis=-1, keepdims=True)
    log_total = top + jnp.log(jnp.sum(jnp.exp(masked - top), axis=-1, keepdims=True))
    positive = jnp.sum(jnp.where(partner > 0.0, logits, 0.0), axis=-1, keepdims=True)
    loss = jnp.sum(log_total - positive, axis=0, keepdims=True) / many
    loss_ref[...] = jnp.broadcast_to(loss, loss_ref.shape)
    grad_raw = LOGIT_SCALE * ((jnp.exp(masked - log_total) - partner) / many)
    grad_raw = grad_raw.astype(BF16)
    turned = jnp.transpose(grad_raw.astype(F32)).astype(BF16)
    grad_embed = dot(grad_raw, embed) + dot(turned, embed)
    inner = jnp.sum(proj * grad_embed, axis=-1, keepdims=True)
    grad_proj = inverse * grad_embed - inverse * inverse * inverse * proj * inner
    grad_proj = grad_proj.astype(BF16)
    pooled_ref[...] = pooled
    grad_proj_ref[...] = grad_proj
    grad_block_ref[...] = dot_nt(grad_proj, w_ref[...]) / counts


def head_kernel(
    dp_size,
    seq_size,
    sums_ref,
    act_ref,
    info_ref,
    w_ref,
    loss_ref,
    pooled_ref,
    grad_proj_ref,
    grad_block_ref,
    act_all_ref,
    near_sums,
    near_act,
    act_total,
    inbox,
    act_inbox,
    near_send,
    near_recv,
    far_send,
    far_recv,
):
    half, groups = seq_size // 2, 2 * dp_size
    dp_at, seq_at = lax.axis_index("dp"), lax.axis_index("seq")
    row, turn = seq_at // half, lax.rem(seq_at, half)
    me = dp_at * 2 + row
    model = sums_ref.shape[1]
    slots = sums_ref.shape[0]

    def member(step):
        return lax.rem(turn + step, half)

    def sibling(step):
        return {"dp": dp_at, "seq": row * half + member(step)}

    def group(step):
        return lax.rem(me + step, groups)

    def peer(step):
        other = group(step)
        return {"dp": other // 2, "seq": lax.rem(other, 2) * half + turn}

    barrier = pltpu.get_barrier_semaphore()
    for step in range(1, half):
        signal(barrier, sibling(step))
    each(1, groups, lambda step: signal(barrier, peer(step)))
    near_sums[turn] = sums_ref[...]
    near_act[turn] = act_ref[...]
    pl.semaphore_wait(barrier, half - 1 + groups - 1)

    def near(step, source):
        return [
            remote(
                buffer.at[source],
                buffer.at[source],
                near_send.at[kind, step],
                near_recv.at[kind, source],
                sibling(step),
            )
            for kind, buffer in enumerate((near_sums, near_act))
        ]

    for step in range(1, half):
        for copy in near(step, turn):
            copy.start()
    for step in range(1, half):
        for copy in near(step, member(step)):
            copy.wait_recv()
    sums, act = near_sums[0], near_act[0]
    for source in range(1, half):
        sums, act = sums + near_sums[source], act + near_act[source]
    info = info_ref[...]
    pooled = sums / (info[:, 0:1] * 64.0 + info[:, 1:2])
    inbox[me] = jnp.concatenate(
        [
            jnp.concatenate([pooled[:, : model // 2], info], axis=1),
            jnp.concatenate([pooled[:, model // 2 :], jnp.zeros_like(info)], axis=1),
        ],
        axis=0,
    ).astype(BF16)
    act_total[...] = act
    act_inbox[me] = act_total[dp_at]

    def message(step, source):
        return remote(
            inbox.at[source], inbox.at[source], far_send.at[0, step], far_recv.at[0, source], peer(step)
        )

    def act_message(step, source):
        return remote(
            act_total.at[group(step) // 2],
            act_inbox.at[source],
            far_send.at[1, step],
            far_recv.at[1, source],
            peer(step),
        )

    each(1, groups, lambda step: message(step, me).start())
    each(1, groups, lambda step: act_message(step, me).start())
    each(1, groups, lambda step: message(step, group(step)).wait_recv())

    loss_terms(inbox, w_ref, slots, loss_ref, pooled_ref, grad_proj_ref, grad_block_ref)
    each(1, groups, lambda step: act_message(step, group(step)).wait_recv())
    act_all_ref[...] = act_inbox[...]
    for step in range(1, half):
        for copy in near(step, turn):
            copy.wait_send()
    each(1, groups, lambda step: message(step, me).wait_send())
    each(1, groups, lambda step: act_message(step, me).wait_send())


def loss_head(sums, act_sums, info, w_proj, dp_size, seq_size):
    slots, model = sums.shape
    groups, half, many = 2 * dp_size, seq_size // 2, 2 * dp_size * slots
    cols = act_sums.shape[1] // dp_size
    act_parts = act_sums.reshape(slots, dp_size, cols).transpose(1, 0, 2)
    vmem = pl.BlockSpec(memory_space=pltpu.VMEM)
    return pl.pallas_call(
        functools.partial(head_kernel, dp_size, seq_size),
        in_specs=[vmem] * 4,
        out_specs=[vmem] * 5,
        out_shape=[
            jax.ShapeDtypeStruct((8, 128), F32),
            jax.ShapeDtypeStruct((many, model), BF16),
            jax.ShapeDtypeStruct((many, w_proj.shape[1]), BF16),
            jax.ShapeDtypeStruct((many, model), F32),
            jax.ShapeDtypeStruct((groups, slots, cols), F32),
        ],
        scratch_shapes=[
            pltpu.VMEM((half, slots, model), F32),
            pltpu.VMEM((half, dp_size, slots, cols), F32),
            pltpu.VMEM((dp_size, slots, cols), F32),
            pltpu.VMEM((groups, 2 * slots, model // 2 + 128), BF16),
            pltpu.VMEM((groups, slots, cols), F32),
            pltpu.SemaphoreType.DMA((2, half)),
            pltpu.SemaphoreType.DMA((2, half)),
            pltpu.SemaphoreType.DMA((2, groups)),
            pltpu.SemaphoreType.DMA((2, groups)),
        ],
        compiler_params=pltpu.CompilerParams(
            collective_id=0, has_side_effects=True, vmem_limit_bytes=40 * MIB
        ),
        cost_estimate=pl.CostEstimate(
            flops=4 * many * model * model, bytes_accessed=8 * MIB, transcendentals=many * many
        ),
        name="loss_head",
    )(sums, act_parts, info, w_proj)


def total_kernel(
    dp_size, seq_size, value_ref, out_ref, seq_box, dp_box, seq_send, seq_recv, dp_send, dp_recv
):
    dp_at, seq_at = lax.axis_index("dp"), lax.axis_index("seq")
    along_seq = lambda step: {"dp": dp_at, "seq": lax.rem(seq_at + step, seq_size)}
    along_dp = lambda step: {"dp": lax.rem(dp_at + step, dp_size), "seq": seq_at}
    barrier = pltpu.get_barrier_semaphore()
    each(1, seq_size, lambda step: signal(barrier, along_seq(step)))
    each(1, dp_size, lambda step: signal(barrier, along_dp(step)))
    pl.semaphore_wait(barrier, seq_size - 1 + dp_size - 1)

    def stage(value, at, size, where, box, send, receive):
        box[at] = value
        copy = lambda step, source: remote(
            box.at[source], box.at[source], send.at[step], receive.at[source], where(step)
        )
        each(1, size, lambda step: copy(step, at).start())
        each(1, size, lambda step: copy(step, lax.rem(at + step, size)).wait_recv())
        total = box[0]
        for source in range(1, size):
            total = total + box[source]
        each(1, size, lambda step: copy(step, at).wait_send())
        return total

    value = stage(value_ref[...], seq_at, seq_size, along_seq, seq_box, seq_send, seq_recv)
    out_ref[...] = stage(value, dp_at, dp_size, along_dp, dp_box, dp_send, dp_recv)


def total_over_all(value, dp_size, seq_size):
    vmem = pl.BlockSpec(memory_space=pltpu.VMEM)
    return pl.pallas_call(
        functools.partial(total_kernel, dp_size, seq_size),
        in_specs=[vmem],
        out_specs=vmem,
        out_shape=jax.ShapeDtypeStruct(value.shape, F32),
        scratch_shapes=[
            pltpu.VMEM((seq_size,) + value.shape, F32),
            pltpu.VMEM((dp_size,) + value.shape, F32),
            pltpu.SemaphoreType.DMA((seq_size,)),
            pltpu.SemaphoreType.DMA((seq_size,)),
            pltpu.SemaphoreType.DMA((dp_size,)),
            pltpu.SemaphoreType.DMA((dp_size,)),
        ],
        compiler_params=pltpu.CompilerParams(collective_id=1, has_side_effects=True),
        name="total_over_all",
    )(value)


def front_kernel(
    tokens_ref,
    seg_ref,
    pair_ref,
    gain_ref,
    wq_hbm,
    wk_hbm,
    wv_hbm,
    qkv_hbm,
    normed_hbm,
    own_hbm,
    row_ref,
    w_own_hbm,
    info_ref,
    column_ref,
    qkv_ref,
    normed_ref,
    w_own_ref,
    x_all,
    seg_here,
    seg_all,
    weights,
    turned,
    w_t,
    load_sem,
    store_sem,
    x_send,
    x_recv,
    seg_send,
    seg_recv,
):
    seq_at = lax.axis_index("seq")
    dp_at = lax.axis_index("dp")
    row, turn = seq_at // 2, lax.rem(seq_at, 2)
    other_core = {"dp": dp_at, "seq": row * 2 + 1 - turn}
    other_chip = {"dp": dp_at, "seq": lax.rem(seq_at + 2, 4)}
    piece, model = x_all.shape[1:]
    width = 64
    halves = piece // TILE
    heads = w_t.shape[0] // (3 * width)
    block_cols = heads // 2 * width
    loads = [
        pltpu.make_async_copy(source, weights.at[at], load_sem.at[at])
        for at, source in enumerate((wq_hbm, wk_hbm, wv_hbm))
    ]
    barrier = pltpu.get_barrier_semaphore()
    signal(barrier, other_core)
    signal(barrier, other_chip)
    for load in loads:
        load.start()
    for at in range(2):
        seg_here[at] = jnp.broadcast_to(seg_ref[at : at + 1, :], seg_here.shape[1:])
    pl.semaphore_wait(barrier, 2)

    def part_of(half):
        return tile_part(half)

    def chip_copy(half, slot):
        return remote(
            tokens_ref.at[1 - row, part_of(half), :],
            x_all.at[slot, part_of(half), :],
            x_send.at[0, half],
            x_recv.at[0, half],
            other_chip,
        )

    def core_copy(kind, half, slot):
        source = tokens_ref.at[row, part_of(half), :] if kind == 1 else x_all.at[slot, part_of(half), :]
        return remote(
            source,
            x_all.at[slot, part_of(half), :],
            x_send.at[kind, half],
            x_recv.at[kind, half],
            other_core,
        )

    def seg_copy(kind, slot):
        source = [seg_here.at[1 - row], seg_here.at[row], seg_all.at[slot]][kind]
        where = other_chip if kind == 0 else other_core
        return remote(source, seg_all.at[slot], seg_send.at[kind], seg_recv.at[kind], where)

    mine, partner = seq_at, lax.rem(seq_at + 2, 4)
    beside, beyond = row * 2 + 1 - turn, lax.rem(row * 2 + 1 - turn + 2, 4)
    for half in range(halves):
        chip_copy(half, mine).start()
    for half in range(halves):
        core_copy(1, half, mine).start()
    seg_copy(0, mine).start()
    seg_copy(1, mine).start()
    x_all[mine] = tokens_ref[row]
    seg_all[mine] = seg_here[row]

    for load in loads:
        load.wait()
    for at in range(3):

        def turn_strip(strip):
            part = tile_part(strip)
            turned[part, :] = jnp.transpose(weights[at, :, part].astype(F32)).astype(BF16)

        each(0, model // TILE, turn_strip)
        for head in range(heads):
            block = head // (heads // 2)
            which = 1 - row if block == 0 else row
            start = pl.multiple_of((which * 2 + turn) * block_cols, block_cols)
            start = start + head % (heads // 2) * width
            w_t[pl.ds((head * 3 + at) * width, width), :] = turned[pl.ds(start, width), :]
    gain = gain_ref[...].reshape(1, model)

    def project(slot, half):
        part = tile_part(half)
        x = x_all[slot, part, :].astype(F32)
        scale = lax.rsqrt(jnp.mean(x * x, axis=1, keepdims=True) + EPS)
        normed_part = jnp.transpose(x * scale * gain).astype(BF16)
        lanes = pl.ds(pl.multiple_of(slot * piece + half * TILE, TILE), TILE)
        normed_ref[:, lanes] = normed_part
        qkv_ref[:, lanes] = dot(w_t[...], normed_part).astype(BF16)

    def results(slot, at):
        lanes = pl.ds(pl.multiple_of(slot * piece, piece), piece)
        return [
            pltpu.make_async_copy(source.at[:, lanes], target.at[:, lanes], store_sem.at[kind, at])
            for kind, (source, target) in enumerate([(qkv_ref, qkv_hbm), (normed_ref, normed_hbm)])
        ]

    order = (mine, beside, partner, beyond)
    own_copies = [
        pltpu.make_async_copy(
            x_all.at[turn + 2 * which], own_hbm.at[pl.ds(which * piece, piece), :], store_sem.at[2, which]
        )
        for which in range(2)
    ] + [pltpu.make_async_copy(w_own_ref, w_own_hbm, store_sem.at[2, 2])]

    def unit(at):
        which, half = at // halves, lax.rem(at, halves)
        slot = jnp.where(which == 0, mine, jnp.where(which == 1, beside, jnp.where(which == 2, partner, beyond)))

        @pl.when(which == 1)
        def _():
            core_copy(1, half, beside).wait_recv()

        @pl.when(at == 2 * halves)
        def _():
            def turn_back(strip):
                part = pl.ds(pl.multiple_of(strip * BLOCK, BLOCK), BLOCK)
                w_own_ref[:, part] = jnp.transpose(w_t[part, :].astype(F32)).astype(BF16)

            each(0, w_t.shape[0] // BLOCK, turn_back)
            own_copies[2].start()
            seg_copy(0, partner).wait_recv()
            seg_copy(2, partner).start()

        @pl.when(which == 2)
        def _():
            chip_copy(half, partner).wait_recv()
            core_copy(2, half, partner).start()

        @pl.when(which == 3)
        def _():
            core_copy(2, half, beyond).wait_recv()

        project(slot, half)

        @pl.when(half == halves - 1)
        def _():
            for copy in results(slot, which):
                copy.start()

    each(0, 4 * halves, unit)
    for copy in own_copies[:2]:
        copy.start()
    seg_copy(1, beside).wait_recv()
    seg_copy(2, beyond).wait_recv()
    slots = info_ref.shape[0]
    ids = lax.broadcasted_iota(jnp.int32, (slots, piece), 0)
    counts = jnp.zeros((slots, 1), F32)
    for slot in range(4):
        row_ref[:, pl.ds(slot * piece, piece)] = seg_all[slot]
        hit = jnp.where(seg_all[slot] == ids, 1.0, 0.0)
        counts = counts + jnp.sum(hit, axis=1, keepdims=True)
    for which in range(2):
        column = jnp.transpose(jnp.broadcast_to(seg_all[turn + 2 * which, 0:1, :].astype(F32), (128, piece)))
        column_ref[pl.ds(which * piece, piece), :] = column.astype(jnp.int32)
    lane = lax.broadcasted_iota(jnp.int32, info_ref.shape, 1)
    own_pairs = jnp.broadcast_to(pair_ref[pl.ds(row, 1), :].astype(F32), (slots, slots))
    square = lax.broadcasted_iota(jnp.int32, (slots, slots), 0)
    square = square == lax.broadcasted_iota(jnp.int32, (slots, slots), 1)
    own_pairs = jnp.sum(jnp.where(square, own_pairs, 0.0), axis=1, keepdims=True)
    high = jnp.floor(counts * (1.0 / 64.0))
    info = jnp.where(lane == 0, high, jnp.where(lane == 1, counts - 64.0 * high, 0.0))
    info_ref[...] = jnp.where(lane == 2, own_pairs, info)
    for half in range(halves):
        chip_copy(half, mine).wait_send()
        core_copy(1, half, mine).wait_send()
        core_copy(2, half, partner).wait_send()
    for kind, slot in enumerate((mine, mine, partner)):
        seg_copy(kind, slot).wait_send()
    for copy in own_copies + [copy for at, slot in enumerate(order) for copy in results(slot, at)]:
        copy.wait()


def gather_and_project(tokens, segment_ids, pair_ids, gain, w_query, w_key, w_value, heads):
    _, piece, model = tokens.shape
    columns, length = 3 * heads * 64, 4 * piece
    vmem, anywhere = pl.BlockSpec(memory_space=pltpu.VMEM), pl.BlockSpec(memory_space=pl.ANY)
    dma = pltpu.SemaphoreType.DMA
    return pl.pallas_call(
        front_kernel,
        in_specs=[vmem] * 4 + [anywhere] * 3,
        out_specs=[anywhere] * 3 + [vmem, anywhere, vmem, vmem],
        out_shape=[
            jax.ShapeDtypeStruct((columns, length), BF16),
            jax.ShapeDtypeStruct((model, length), BF16),
            jax.ShapeDtypeStruct((2 * piece, model), BF16),
            jax.ShapeDtypeStruct((8, length), jnp.int32),
            jax.ShapeDtypeStruct((model, columns), BF16),
            jax.ShapeDtypeStruct((pair_ids.shape[1], 128), F32),
            jax.ShapeDtypeStruct((2 * piece, 128), jnp.int32),
        ],
        scratch_shapes=[
            pltpu.VMEM((columns, length), BF16),
            pltpu.VMEM((model, length), BF16),
            pltpu.VMEM((model, columns), BF16),
            pltpu.VMEM((4, piece, model), BF16),
            pltpu.VMEM((2, 8, piece), jnp.int32),
            pltpu.VMEM((4, 8, piece), jnp.int32),
            pltpu.VMEM((3, model, model), BF16),
            pltpu.VMEM((model, model), BF16),
            pltpu.VMEM((columns, model), BF16),
            dma((3,)),
            dma((3, 4)),
            dma((3, piece // TILE)),
            dma((3, piece // TILE)),
            dma((3,)),
            dma((3,)),
        ],
        compiler_params=pltpu.CompilerParams(
            collective_id=5, has_side_effects=True, vmem_limit_bytes=63 * MIB
        ),
        cost_estimate=pl.CostEstimate(
            flops=2 * columns * length * model, bytes_accessed=20 * MIB, transcendentals=0
        ),
        name="gather_and_project",
    )(
        tokens,
        segment_ids,
        pair_ids,
        gain,
        w_query,
        w_key,
        w_value,
    )


def middle_kernel(
    dp_size,
    info_ref,
    seg_ref,
    gain_ref,
    w_out_hbm,
    x_hbm,
    w_up_hbm,
    w_down_hbm,
    w_proj_hbm,
    o_hbm,
    mixed_ref,
    loss_ref,
    pooled_ref,
    grad_proj_ref,
    grad_block_ref,
    act_all_ref,
    g_ref,
    grad_hbm,
    gain_sum,
    up_ref,
    out_ref,
    w_out,
    x_own,
    w_up,
    w_down,
    w_proj,
    attended,
    hidden,
    normed_two,
    normed_t,
    act,
    slope,
    total,
    members_t,
    sum_parts,
    mixed_out,
    near_sums,
    near_act,
    act_total,
    inbox,
    act_inbox,
    grad_b,
    grad_att,
    out_send,
    out_recv,
    load_sem,
    store_sem,
    head_load,
    head_send,
    head_recv,
    near_send,
    near_recv,
    far_send,
    far_recv,
    mixed_send,
    mixed_recv,
    att_send,
    att_recv,
    core_send,
    core_recv,
):
    dp_at, seq_at = lax.axis_index("dp"), lax.axis_index("seq")
    row, turn = seq_at // 2, lax.rem(seq_at, 2)
    groups, me = 2 * dp_size, dp_at * 2 + row
    other_core = {"dp": dp_at, "seq": row * 2 + 1 - turn}
    other_chip = {"dp": dp_at, "seq": lax.rem(seq_at + 2, 4)}
    group = lambda step: lax.rem(me + step, groups)
    peer = lambda step: {"dp": group(step) // 2, "seq": lax.rem(group(step), 2) * 2 + turn}
    tokens, model = hidden.shape
    slots = info_ref.shape[0]
    piece, units = tokens // 2, w_up.shape[1]
    cols, out_cols = up_ref.shape[2], out_ref.shape[2]
    act_cols = units // dp_size
    pairs = [
        (w_out_hbm, w_out),
        (x_hbm, x_own),
        (w_up_hbm, w_up),
        (w_down_hbm, w_down),
        (w_proj_hbm, w_proj),
    ]
    loads = [pltpu.make_async_copy(*pair, load_sem.at[at]) for at, pair in enumerate(pairs)]
    barrier = pltpu.get_barrier_semaphore()
    signal(barrier, other_core)
    each(1, groups, lambda step: signal(barrier, peer(step)))

    def head_rows(member, block):
        which = 1 - row if block == 0 else row
        return pl.ds(pl.multiple_of((which * 2 + member) * out_cols, out_cols), out_cols)

    def row_lanes(member, half):
        return pl.ds(pl.multiple_of((member + 2 * half) * piece, piece), piece)

    def half_of(half):
        return pl.ds(pl.multiple_of(half * piece, piece), piece)

    def heads_here(block, half):
        return pltpu.make_async_copy(
            o_hbm.at[pl.ds(block * out_cols, out_cols), row_lanes(turn, half)],
            attended.at[head_rows(turn, block), half_of(half)],
            head_load.at[block, half],
        )

    def heads_there(block, half, sender):
        return remote(
            o_hbm.at[pl.ds(block * out_cols, out_cols), row_lanes(1 - sender, half)],
            attended.at[head_rows(sender, block), half_of(half)],
            head_send.at[block, half],
            head_recv.at[block, half],
            other_core,
        )

    quarters = [(block, half) for half in range(2) for block in range(2)]
    for block, half in quarters:
        heads_here(block, half).start()
    for load in loads:
        load.start()
    pl.semaphore_wait(barrier, groups)
    for block, half in quarters:
        heads_there(block, half, turn).start()

    def members(rows, parts):
        seg = seg_ref[rows, :]
        lane = lax.broadcasted_iota(jnp.int32, seg.shape, 1)
        hit = (lax.rem(lane, 16) == seg) & (lane < 16 * parts)
        return jnp.where(hit, 1.0, 0.0)

    gain = gain_ref[...].reshape(1, model)
    loads[0].wait()
    loads[1].wait()
    per_half = piece // TILE

    def attended_tile(at):
        @pl.when(lax.rem(at, per_half) == 0)
        def _():
            for block in range(2):
                heads_here(block, at // per_half).wait()
                heads_there(block, at // per_half, 1 - turn).wait_recv()

        rows = tile_part(at)
        left = jnp.transpose(attended[:, rows].astype(F32)).astype(BF16)
        value = x_own[rows, :].astype(F32) + dot(left, w_out[...])
        hidden[rows, :] = value
        scale = lax.rsqrt(jnp.mean(value * value, axis=1, keepdims=True) + EPS)
        value = value * scale * gain
        normed_two[rows, :] = value.astype(BF16)
        normed_t[:, rows] = jnp.transpose(value).astype(BF16)

    each(0, tokens // TILE, attended_tile)
    loads[2].wait()

    def up(at):
        lanes = tile_part(at)
        for half in range(2):
            rows = half_of(half)
            value = dot(normed_two[rows, :], w_up[:, lanes])
            below = 0.5 + 0.5 * lax.erf(value * (0.5**0.5))
            density = jnp.exp(-0.5 * value * value) * 0.3989422804014327
            act[rows, lanes] = (value * below).astype(BF16)
            slope[rows, lanes] = (below + value * density).astype(BF16)

    each(0, units // TILE, up)
    loads[3].wait()
    member = jnp.transpose(members(pl.ds(0, tokens), 1))[:16].astype(BF16)
    sum_parts[...] = jnp.zeros_like(sum_parts)

    def down(half):
        rows = pl.ds(pl.multiple_of(half * piece, piece), piece)
        value = hidden[rows, :] + dot(act[rows, :], w_down[...])
        total[rows, :] = value
        high = value.astype(BF16)
        rest = (value - high.astype(F32)).astype(BF16)
        left = members_t[:, rows]
        sum_parts[...] += dot(left, high) + dot(left, rest)

    members_t[...] = member
    each(0, 2, down)
    near_sums[turn] = sum_parts[:slots, :]

    def act_part(part):
        lanes = pl.ds(pl.multiple_of(part * act_cols, act_cols), act_cols)
        near_act[turn, part] = dot(members_t[...], act[:, lanes])[:slots]

    each(0, dp_size, act_part)

    def near(source):
        return [
            remote(
                buffer.at[source],
                buffer.at[source],
                near_send.at[kind],
                near_recv.at[kind],
                other_core,
            )
            for kind, buffer in enumerate((near_sums, near_act))
        ]

    for copy in near(turn):
        copy.start()
    mixed_ref[row] = total[pl.ds(pl.multiple_of(row * piece, piece), piece), :].astype(BF16)
    mixed_out[...] = total[pl.ds(pl.multiple_of((1 - row) * piece, piece), piece), :].astype(BF16)
    mixed_copy = lambda at: remote(
        mixed_out, mixed_ref.at[at], mixed_send.at[0], mixed_recv.at[0], other_chip
    )
    for copy in near(1 - turn):
        copy.wait_recv()
    info = info_ref[...]
    pooled = (near_sums[0] + near_sums[1]) / (info[:, 0:1] * 64.0 + info[:, 1:2])
    inbox[me] = jnp.concatenate(
        [
            jnp.concatenate([pooled[:, : model // 2], info], axis=1),
            jnp.concatenate([pooled[:, model // 2 :], jnp.zeros_like(info)], axis=1),
        ],
        axis=0,
    ).astype(BF16)

    def message(step, source):
        return remote(
            inbox.at[source], inbox.at[source], far_send.at[0, step], far_recv.at[0, source], peer(step)
        )

    def act_message(step, source):
        return remote(
            act_total.at[group(step) // 2],
            act_inbox.at[source],
            far_send.at[1, step],
            far_recv.at[1, source],
            peer(step),
        )

    each(1, groups, lambda step: message(step, me).start())
    act_total[...] = near_act[0] + near_act[1]
    act_inbox[me] = act_total[dp_at]
    loads[4].wait()
    each(1, groups, lambda step: message(step, group(step)).wait_recv())
    each(1, groups, lambda step: act_message(step, me).start())
    mixed_copy(row).start()
    loss_terms(inbox, w_proj, slots, loss_ref, pooled_ref, grad_proj_ref, grad_block_ref)

    def stacked(parts):
        parts = [part.astype(BF16) for part in parts]
        rest = jnp.zeros((128 - 16 * len(parts), parts[0].shape[1]), BF16)
        return jnp.concatenate(parts + [rest], axis=0)

    block = grad_block_ref[pl.ds(pl.multiple_of(me * slots, slots), slots), :]
    block = jnp.concatenate([block, jnp.zeros_like(block)], axis=0)
    block_b, block_parts = block.astype(BF16), stacked(three_parts(block))

    def grad_up(at):
        lanes = tile_part(at)
        grad_act = dot_nt(block_b, w_down[lanes, :])
        high = grad_act.astype(BF16).astype(F32)
        both = stacked([high, grad_act - high])
        for half in range(2):
            rows = half_of(half)
            spread = dot(members(rows, 2).astype(BF16), both)
            slope[rows, lanes] = (spread * slope[rows, lanes].astype(F32)).astype(BF16)

    each(0, units // TILE, grad_up)
    gain_sum[...] = jnp.zeros_like(gain_sum)

    def token_part(at):
        rows = pl.ds(pl.multiple_of(at * BLOCK, BLOCK), BLOCK)
        grad, value = total[rows, :], hidden[rows, :]
        scale = lax.rsqrt(jnp.mean(value * value, axis=1, keepdims=True) + EPS)
        scaled = gain * grad
        inner = jnp.mean(scaled * value, axis=1, keepdims=True)
        terms = grad * value * scale
        gain_sum[...] += jnp.sum(terms.reshape(BLOCK // 8, 8, model), axis=0)
        result = dot(members(rows, 3).astype(BF16), block_parts)
        result = result + scale * scaled - value * (scale * scale * scale * inner)
        total[rows, :] = result
        grad_b[rows, :] = result.astype(BF16)

    def att_copy(block, half, sender):
        return remote(
            grad_att.at[head_rows(1 - sender, block), half_of(half)],
            g_ref.at[pl.ds(block * out_cols, out_cols), row_lanes(sender, half)],
            att_send.at[block, half],
            att_recv.at[block, half],
            other_core,
        )

    def store(half):
        return pltpu.make_async_copy(
            total.at[half_of(half), :], grad_hbm.at[half_of(half), :], store_sem.at[half]
        )

    def token_half(half):
        rows = half_of(half)
        total[rows, :] = dot_nt(slope[rows, :], w_up[...])
        each(half * (piece // BLOCK), (half + 1) * (piece // BLOCK), token_part)
        store(half).start()
        grad_att[:, rows] = dot_nt(w_out[...], grad_b[rows, :]).astype(BF16)
        for block in range(2):
            att_copy(block, half, turn).start()

    each(0, 2, token_half)
    for block, half in quarters:
        mine = grad_att[head_rows(turn, block), half_of(half)]
        g_ref[pl.ds(block * out_cols, out_cols), row_lanes(turn, half)] = mine

    def up_box(kind, x):
        return act.at[pl.ds(0, model), pl.ds(pl.multiple_of((2 * kind + x) * cols, cols), cols)]

    def up_copy(x):
        return remote(up_box(0, x), up_box(1, x), core_send.at[0, x], core_recv.at[0, x], other_core)

    def out_copy(x):
        return remote(
            out_send.at[x], out_recv.at[x], core_send.at[1, x], core_recv.at[1, x], other_core
        )

    def out_part(x, core):
        starts = [(2 * x + side) * out_cols for side in range(2)]
        return jnp.where(core == 0, *(out_full[:, start : start + out_cols] for start in starts))

    strips = cols // TILE

    def up_strip(at):
        side, x = at // (2 * strips), lax.rem(at // strips, 2)
        strip = lax.rem(at, strips)
        core = jnp.where(side == 0, 1 - turn, turn)
        start = pl.multiple_of((2 * x + core) * cols + strip * TILE, TILE)
        value = dot(normed_t[...], slope[:, pl.ds(start, TILE)]).astype(BF16)

        @pl.when(side == 0)
        def _():
            act[:model, pl.ds(pl.multiple_of(x * cols + strip * TILE, TILE), TILE)] = value

            @pl.when(strip == strips - 1)
            def _():
                up_copy(x).start()

        @pl.when(side == 1)
        def _():
            up_ref[x, :, tile_part(strip)] = value

    each(0, 2 * strips, up_strip)
    out_full = dot(attended[...], grad_b[...])
    for x in range(2):
        out_send[x] = out_part(x, 1 - turn).astype(BF16)
        out_copy(x).start()
    each(2 * strips, 4 * strips, up_strip)
    for x in range(2):
        up_copy(x).wait_recv()
        out_copy(x).wait_recv()
        up_ref[x] = added(up_ref[x], act[:model, (2 + x) * cols : (3 + x) * cols])
        out_ref[x] = (out_part(x, turn) + out_recv[x].astype(F32)).astype(BF16)

    mixed_copy(1 - row).wait_recv()
    each(1, groups, lambda step: act_message(step, group(step)).wait_recv())
    act_all_ref[...] = act_inbox[...]
    for block, half in quarters:
        att_copy(block, half, 1 - turn).wait_recv()
        att_copy(block, half, turn).wait_send()
        heads_there(block, half, turn).wait_send()
    for x in range(2):
        up_copy(x).wait_send()
        out_copy(x).wait_send()
    for copy in near(turn):
        copy.wait_send()
    mixed_copy(row).wait_send()
    each(1, groups, lambda step: message(step, me).wait_send())
    each(1, groups, lambda step: act_message(step, me).wait_send())
    for half in range(2):
        store(half).wait()


def feed_forward_and_loss(info, seg_columns, gain, w_out, x_own, w_up, w_down, w_proj, o_t, dp_size):
    slots = info.shape[0]
    tokens, model = x_own.shape
    units, piece = w_up.shape[1], tokens // 2
    cols, out_cols = units // 4, model // 4
    groups, many, act_cols = 2 * dp_size, 2 * dp_size * slots, units // dp_size
    vmem, anywhere = pl.BlockSpec(memory_space=pltpu.VMEM), pl.BlockSpec(memory_space=pl.ANY)
    dma, shape = pltpu.SemaphoreType.DMA, jax.ShapeDtypeStruct
    return pl.pallas_call(
        functools.partial(middle_kernel, dp_size),
        in_specs=[vmem] * 3 + [anywhere] * 6,
        out_specs=[vmem] * 7 + [anywhere] + [vmem] * 3,
        out_shape=[
            shape((2, piece, model), BF16),
            shape((8, 128), F32),
            shape((many, model), BF16),
            shape((many, w_proj.shape[1]), BF16),
            shape((many, model), F32),
            shape((groups, slots, act_cols), F32),
            shape((2 * out_cols, 2 * tokens), BF16),
            shape((tokens, model), F32),
            shape((8, model), F32),
            shape((2, model, cols), BF16),
            shape((2, model, out_cols), BF16),
        ],
        scratch_shapes=[
            pltpu.VMEM((model, model), BF16),
            pltpu.VMEM((tokens, model), BF16),
            pltpu.VMEM((model, units), BF16),
            pltpu.VMEM((units, model), BF16),
            pltpu.VMEM(w_proj.shape, BF16),
            pltpu.VMEM((model, tokens), BF16),
            pltpu.VMEM((tokens, model), F32),
            pltpu.VMEM((tokens, model), BF16),
            pltpu.VMEM((model, tokens), BF16),
            pltpu.VMEM((tokens, units), BF16),
            pltpu.VMEM((tokens, units), BF16),
            pltpu.VMEM((tokens, model), F32),
            pltpu.VMEM((16, tokens), BF16),
            pltpu.VMEM((16, model), F32),
            pltpu.VMEM((piece, model), BF16),
            pltpu.VMEM((2, slots, model), F32),
            pltpu.VMEM((2, dp_size, slots, act_cols), F32),
            pltpu.VMEM((dp_size, slots, act_cols), F32),
            pltpu.VMEM((groups, 2 * slots, model // 2 + 128), BF16),
            pltpu.VMEM((groups, slots, act_cols), F32),
            pltpu.VMEM((tokens, model), BF16),
            pltpu.VMEM((model, tokens), BF16),
            pltpu.VMEM((2, model, out_cols), BF16),
            pltpu.VMEM((2, model, out_cols), BF16),
            dma((5,)),
            dma((2,)),
            dma((2, 2)),
            dma((2, 2)),
            dma((2, 2)),
            dma((2,)),
            dma((2,)),
            dma((2, groups)),
            dma((2, groups)),
            dma((1,)),
            dma((1,)),
            dma((2, 2)),
            dma((2, 2)),
            dma((2, 2)),
            dma((2, 2)),
        ],
        compiler_params=pltpu.CompilerParams(
            collective_id=4, has_side_effects=True, vmem_limit_bytes=63 * MIB
        ),
        cost_estimate=pl.CostEstimate(
            flops=8 * units * tokens * model,
            bytes_accessed=24 * MIB,
            transcendentals=2 * tokens * units,
        ),
        name="feed_forward_and_loss",
    )(
        info,
        seg_columns,
        gain,
        w_out,
        x_own,
        w_up,
        w_down,
        w_proj,
        o_t,
    )


def tail_kernel(
    dp_size,
    bucket_count,
    gain_ref,
    ffn_ref,
    last_ref,
    late_ref,
    pooled_ref,
    proj_ref,
    block_ref,
    act_ref,
    diag_ref,
    w_hbm,
    d_hbm,
    x_hbm,
    hidden_hbm,
    own_ref,
    chip_in,
    total_ref,
    g_qkv_ref,
    g_proj_ref,
    g_down_ref,
    w_ref,
    d_ref,
    x_ref,
    hidden_ref,
    near_out,
    near_in,
    part,
    gain_sum,
    chip_out,
    last_far,
    turned,
    seq_box,
    dp_box,
    load_sem,
    near_send,
    near_recv,
    chip_send,
    chip_recv,
    last_send,
    last_recv,
    seq_send,
    seq_recv,
    dp_send,
    dp_recv,
):
    seq_size = 4
    dp_at, seq_at = lax.axis_index("dp"), lax.axis_index("seq")
    row, turn = seq_at // 2, lax.rem(seq_at, 2)
    along_seq = lambda step: {"dp": dp_at, "seq": lax.rem(seq_at + step, seq_size)}
    along_dp = lambda step: {"dp": lax.rem(dp_at + step, dp_size), "seq": seq_at}
    other_core = {"dp": dp_at, "seq": row * 2 + 1 - turn}
    other_chip = {"dp": dp_at, "seq": lax.rem(seq_at + 2, seq_size)}
    model, piece = w_ref.shape[0], own_ref.shape[0]
    rows = g_proj_ref.shape[0]
    parts = TILE // BLOCK
    barrier = pltpu.get_barrier_semaphore()
    each(1, seq_size, lambda step: signal(barrier, along_seq(step)))
    each(1, dp_size, lambda step: signal(barrier, along_dp(step)))
    loads = [
        pltpu.make_async_copy(source, target, load_sem.at[at])
        for at, (source, target) in enumerate(
            [(w_hbm, w_ref), (d_hbm, d_ref), (x_hbm, x_ref), (hidden_hbm, hidden_ref)]
        )
    ]
    for load in loads:
        load.start()

    def product(member, at):
        which = jnp.where(at < 2, 1 - row, row)
        start = pl.multiple_of((member + 2 * which) * piece + lax.rem(at, 2) * TILE, TILE)
        return dot(w_ref[...], d_ref[:, pl.ds(start, TILE)])

    def near_copy(at):
        return remote(near_out.at[at], near_in.at[at], near_send.at[at], near_recv.at[at], other_core)

    def chip_copy(at):
        return remote(chip_out.at[at], chip_in.at[at], chip_send.at[at], chip_recv.at[at], other_chip)

    def last_copy(step, source):
        to = pl.ds(pl.multiple_of(lax.rem(dp_at + step, dp_size) * rows, rows), rows)
        return remote(
            last_ref.at[to, :], last_far.at[source], last_send.at[step], last_recv.at[source], along_dp(step)
        )

    gain_sum[...] = jnp.zeros_like(gain_sum)
    gain = gain_ref[...].reshape(1, model)
    loads[0].wait()
    loads[1].wait()
    def quarter(at):
        near_out[at] = product(1 - turn, at).astype(BF16)

        @pl.when(at == 0)
        def _():
            pl.semaphore_wait(barrier, seq_size - 1 + dp_size - 1)

        near_copy(at).start()
        part[...] = product(turn, at)

        @pl.when(at == 0)
        def _():
            each(1, dp_size, lambda step: last_copy(step, dp_at).start())
            loads[2].wait()
            loads[3].wait()

        near_copy(at).wait_recv()
        which = jnp.where(at < 2, 1 - row, row)

        def block(sub):
            lanes = pl.ds(pl.multiple_of(sub * BLOCK, BLOCK), BLOCK)
            place = pl.multiple_of(lax.rem(at, 2) * TILE + sub * BLOCK, BLOCK)
            there = pl.ds(pl.multiple_of(which * piece + place, BLOCK), BLOCK)
            grad = jnp.transpose(part[:, lanes] + near_in[at, :, lanes].astype(F32))
            x = x_ref[there, :].astype(F32)
            scale = lax.rsqrt(jnp.mean(x * x, axis=1, keepdims=True) + EPS)
            scaled = gain * grad
            inner = jnp.mean(scaled * x, axis=1, keepdims=True)
            gain_sum[...] += jnp.sum((grad * x * scale).reshape(BLOCK // 8, 8, model), axis=0)
            result = hidden_ref[there, :] + scale * scaled - x * (scale * scale * scale * inner)

            @pl.when(at < 2)
            def _():
                chip_out[at * parts + sub] = result.astype(BF16)
                chip_copy(at * parts + sub).start()

            @pl.when(at >= 2)
            def _():
                own_ref[pl.ds(place, BLOCK), :] = result

        each(0, parts, block)

    each(0, 4, quarter)

    heads = diag_ref.shape[0]
    sums = diag_ref[...].reshape(heads * 8, 2 * BLOCK)
    sums = [value.astype(BF16) for value in three_parts(sums)]
    row_at = lax.rem(lax.broadcasted_iota(jnp.int32, (heads * 8, 128), 0), 8)
    lane = lax.broadcasted_iota(jnp.int32, (2 * BLOCK, 128), 1)
    place = lax.broadcasted_iota(jnp.int32, (2 * BLOCK, 128), 0)
    place = jnp.where(place < BLOCK, place, place - 2 * BLOCK)
    table = jnp.zeros((heads * 8, 128), F32)
    for band in range(BANDS):
        offset = (band - BANDS // 2) * BLOCK - place
        onehot = jnp.where(bucket_of(offset, bucket_count // 2) == lane, 1.0, 0.0).astype(BF16)
        found = dot(sums[0], onehot) + dot(sums[1], onehot) + dot(sums[2], onehot)
        table = table + jnp.where(row_at == band, found, 0.0)
    table = jnp.sum(table.reshape(heads, 8, 128), axis=1)
    run = heads // 2
    table = jnp.concatenate(
        [
            jnp.where(
                (1 - row) * 2 + turn == group,
                table[:run],
                jnp.where(row * 2 + turn == group, table[run:], 0.0),
            )
            for group in range(4)
        ],
        axis=0,
    )

    def as_rows(value):
        value = jnp.sum(value, axis=0, keepdims=True)
        return [value[:, at : at + 128] for at in range(0, model, 128)]

    value = jnp.concatenate(as_rows(gain_sum[...]) + as_rows(ffn_ref[...]) + [table], axis=0)

    def stage_total(value, at, size, where, box, send, receive):
        box[at] = value
        copy = lambda step, source: remote(
            box.at[source], box.at[source], send.at[step], receive.at[source], where(step)
        )
        each(1, size, lambda step: copy(step, at).start())
        each(1, size, lambda step: copy(step, lax.rem(at + step, size)).wait_recv())
        total = box[0]
        for source in range(1, size):
            total = total + box[source]
        each(1, size, lambda step: copy(step, at).wait_send())
        return total

    value = stage_total(value, seq_at, seq_size, along_seq, seq_box, seq_send, seq_recv)
    total_ref[...] = stage_total(value, dp_at, dp_size, along_dp, dp_box, dp_send, dp_recv)

    own_rows = pl.ds(pl.multiple_of(dp_at * rows, rows), rows)
    out_cols = g_proj_ref.shape[1]
    own_cols = pl.ds(pl.multiple_of(seq_at * out_cols, out_cols), out_cols)
    turned[0] = jnp.transpose(pooled_ref[...].astype(F32))
    turned[1] = jnp.transpose(proj_ref[...].astype(F32))
    turned[2] = jnp.transpose(block_ref[...])
    g_proj_ref[...] = dot_nt(turned[0, own_rows, :].astype(BF16), turned[1, own_cols, :].astype(BF16))
    act = jnp.transpose(act_ref[...].reshape(pooled_ref.shape[0], act_ref.shape[2]))
    block = turned[2, own_cols, :].astype(BF16)
    high = act.astype(BF16)
    rest = (act - high.astype(F32)).astype(BF16)
    g_down_ref[...] = dot_nt(high, block) + dot_nt(rest, block)

    each(1, dp_size, lambda step: last_copy(step, lax.rem(dp_at + step, dp_size)).wait_recv())
    last_far[dp_at] = jnp.zeros(last_far.shape[1:], BF16)
    last = last_ref[own_rows, :].astype(F32)
    for source in range(dp_size):
        last = last + last_far[source].astype(F32)
    late = [late_ref[which] for which in range(late_ref.shape[0])] + [last]
    width = late_ref.shape[2] // 3
    for kind in range(3):
        g_qkv_ref[kind] = jnp.concatenate(
            [value[:, kind * width : (kind + 1) * width] for value in late], axis=1
        )
    for at in range(2 * parts):
        chip_copy(at).wait_recv()
    for at in range(4):
        near_copy(at).wait_send()
    for at in range(2 * parts):
        chip_copy(at).wait_send()
    each(1, dp_size, lambda step: last_copy(step, dp_at).wait_send())


def token_gradients(
    d_qkv, w_qkv, x_own, grad_hidden, gain, gain_ffn, last, late, pooled, proj, block, act, diag, buckets, dp_size
):
    tokens, model = x_own.shape
    piece, many = tokens // 2, pooled.shape[0]
    rows, out_cols = model // dp_size, model // 4
    run, width = late.shape[0] + 1, late.shape[2] // 3
    vmem, anywhere = pl.BlockSpec(memory_space=pltpu.VMEM), pl.BlockSpec(memory_space=pl.ANY)
    dma, shape = pltpu.SemaphoreType.DMA, jax.ShapeDtypeStruct
    return pl.pallas_call(
        functools.partial(tail_kernel, dp_size, buckets),
        in_specs=[vmem] * 9 + [anywhere] * 4,
        out_specs=[vmem] * 6,
        out_shape=[
            shape((piece, model), F32),
            shape((piece // BLOCK, BLOCK, model), BF16),
            shape((24, 128), F32),
            shape((3, rows, run * width), F32),
            shape((rows, out_cols), F32),
            shape((act.shape[2], out_cols), F32),
        ],
        scratch_shapes=[
            pltpu.VMEM(w_qkv.shape, BF16),
            pltpu.VMEM(d_qkv.shape, BF16),
            pltpu.VMEM(x_own.shape, BF16),
            pltpu.VMEM(grad_hidden.shape, F32),
            pltpu.VMEM((4, model, TILE), BF16),
            pltpu.VMEM((4, model, TILE), BF16),
            pltpu.VMEM((model, TILE), F32),
            pltpu.VMEM((8, model), F32),
            pltpu.VMEM((piece // BLOCK, BLOCK, model), BF16),
            pltpu.VMEM((dp_size, rows, last.shape[1]), BF16),
            pltpu.VMEM((3, model, many), F32),
            pltpu.VMEM((4, 24, 128), F32),
            pltpu.VMEM((dp_size, 24, 128), F32),
            dma((4,)),
            dma((4,)),
            dma((4,)),
            dma((piece // BLOCK,)),
            dma((piece // BLOCK,)),
            dma((dp_size,)),
            dma((dp_size,)),
            dma((4,)),
            dma((4,)),
            dma((dp_size,)),
            dma((dp_size,)),
        ],
        compiler_params=pltpu.CompilerParams(
            collective_id=3, has_side_effects=True, vmem_limit_bytes=63 * MIB
        ),
        cost_estimate=pl.CostEstimate(
            flops=2 * d_qkv.shape[0] * d_qkv.shape[1] * model,
            bytes_accessed=16 * MIB,
            transcendentals=0,
        ),
        name="token_gradients",
    )(
        gain,
        gain_ffn,
        last,
        late,
        pooled,
        proj,
        block,
        act,
        diag,
        w_qkv,
        d_qkv,
        x_own,
        grad_hidden,
    )


def normed(inputs, gain_vec):
    return inputs * lax.rsqrt(jnp.mean(inputs * inputs, axis=-1, keepdims=True) + EPS) * gain_vec


def norm_back(inputs, gain_vec, grads_in):
    scale = lax.rsqrt(jnp.mean(inputs * inputs, axis=-1, keepdims=True) + EPS)
    gain_grad = jnp.sum(grads_in * inputs * scale, axis=0)
    scaled = gain_vec * grads_in
    inner = jnp.mean(scaled * inputs, axis=-1, keepdims=True)
    return scale * scaled - inputs * (scale * scale * scale * inner), gain_grad


def on_device(
    tokens,
    segment_ids,
    pair_ids,
    w_query,
    w_key,
    w_value,
    w_out,
    w_up,
    w_down,
    w_proj,
    gain_attn,
    gain_ffn,
    rel_bias,
):
    _, piece, model_width = tokens.shape
    bucket_count, head_count = rel_bias.shape
    slots = pair_ids.shape[1]
    dp_size, seq_size = lax.axis_size("dp"), lax.axis_size("seq")
    half = seq_size // 2
    length = piece * seq_size
    heads = head_count // half
    width = model_width // head_count
    dp_at, seq_at = lax.axis_index("dp"), lax.axis_index("seq")
    row, turn = seq_at // half, lax.rem(seq_at, half)
    across = [(i, (i + half) % seq_size) for i in range(seq_size)]

    def by_row(own, other):
        return jnp.where(row == 0, own, other), jnp.where(row == 0, other, own)

    def among(step):
        return [(i, i // half * half + (i % half + step) % half) for i in range(seq_size)]

    def trade(own, send_to):
        entries = [own] * half
        for step in range(1, half):
            got = lax.ppermute(send_to(lax.rem(turn + step, half)), "seq", among(step))
            source = lax.rem(turn + half - step, half)
            entries = [jnp.where(source == j, got, entry) for j, entry in enumerate(entries)]
        return entries

    def pick(value, at, size, dim):
        return lax.dynamic_slice_in_dim(value, at * size, size, dim)

    def pieces_of(value, member, dim):
        return jnp.concatenate(
            [pick(value, member, piece, dim), pick(value, member + half, piece, dim)], axis=dim
        )

    def in_row_order(entries, dim):
        halves = [jnp.split(entry, 2, axis=dim) for entry in entries]
        return jnp.concatenate([pair[0] for pair in halves] + [pair[1] for pair in halves], axis=dim)

    def own_pieces(local):
        own = lax.dynamic_index_in_dim(local, row, 0, keepdims=False)
        other = lax.dynamic_index_in_dim(local, 1 - row, 0, keepdims=False)
        return jnp.concatenate(by_row(own, lax.ppermute(other, "seq", across)), axis=0)

    def whole_row(pair):
        return in_row_order(trade(pair, lambda member: pair), 0)

    def hand_back(pair, kind):
        own, other = pick(pair, row, piece, 0), pick(pair, 1 - row, piece, 0)
        return jnp.stack(by_row(own, lax.ppermute(other.astype(kind), "seq", across).astype(own.dtype)))

    aligned = seq_size == 4 and heads % 2 == 0
    blocks = 2 if aligned else 1
    block_heads = heads // blocks
    columns, block_columns = heads * width, block_heads * width

    def block_at(block):
        return (1 - row if block == 0 else row) if aligned else 0

    def cut(value, member, size, dim):
        parts = [pick(value, block_at(block) * half + member, size, dim) for block in range(blocks)]
        return jnp.concatenate(parts, axis=dim)

    if aligned:
        qkv_t, normed_t, x_pair, seg_row, w_own, info, seg_columns = gather_and_project(
            tokens, segment_ids, pair_ids, gain_attn, w_query, w_key, w_value, heads
        )
    else:
        x_pair, seg_own = own_pieces(tokens), own_pieces(segment_ids)
        x_row, seg_row = whole_row(x_pair), whole_row(seg_own)[None]
        w_qkv = [cut(weight, turn, block_columns, 1) for weight in (w_query, w_key, w_value)]
        w_qkv = [weight.reshape(model_width, heads, width) for weight in w_qkv]
        w_qkv = jnp.stack(w_qkv, axis=2).reshape(model_width, 3 * columns)
        normed_one = normed(x_row.astype(F32), gain_attn).astype(BF16)
        qkv_t = jnp.einsum("dc,td->ct", w_qkv, normed_one, preferred_element_type=F32).astype(BF16)
        x_own = x_pair.astype(F32)
        slot_ids = jnp.arange(slots, dtype=jnp.int32)
        counts = jnp.sum((seg_row == slot_ids[:, None]).astype(jnp.int32), axis=1)
        own_pairs = lax.dynamic_index_in_dim(pair_ids, row, 0, keepdims=False)
        info = jnp.stack([counts // 64, counts % 64, own_pairs], axis=1).astype(F32)
        info = jnp.concatenate([info, jnp.zeros((slots, 125), F32)], axis=1)
    qkv_t = qkv_t.reshape(heads, 3, width, length)
    table = cut(rel_bias, turn, block_heads, 1)
    onehot = (
        bucket_of(diagonal_offsets(), bucket_count // 2)[:, :, None]
        == jnp.arange(bucket_count, dtype=jnp.int32)
    ).astype(F32)
    diag = jnp.einsum("txb,bh->htx", onehot, table, precision=lax.Precision.HIGHEST)
    diag = jnp.concatenate([diag, jnp.zeros((heads, 8 - BANDS, 2 * BLOCK), F32)], axis=1)
    o_t, o_b, inverse, probs = attention_forward(slots, qkv_t, seg_row, diag)

    def heads_to_tokens(value):
        entries = trade(pieces_of(value, turn, 1), lambda member: pieces_of(value, member, 1))
        parts = [jnp.split(entry, blocks, axis=0) for entry in entries]
        if aligned:
            parts = [by_row(part[1], part[0]) for part in parts]
        return jnp.concatenate([part[block] for block in range(blocks) for part in parts], axis=0)

    def tokens_to_heads(value):
        own = cut(value, turn, block_columns, 0)
        return in_row_order(trade(own, lambda member: cut(value, member, block_columns, 0)), 1)

    if aligned:
        (
            mixed,
            loss,
            pooled,
            grad_proj,
            grad_block_all,
            every_act,
            g_t,
            grad_hidden,
            grad_gain_ffn,
            up_sum,
            out_sum,
        ) = feed_forward_and_loss(
            info,
            seg_columns,
            gain_ffn,
            w_out,
            x_pair,
            w_up,
            w_down,
            w_proj,
            o_b.reshape(columns, length),
            dp_size,
        )
        d_qkv, diag_grads, g_up, g_out, late, last = attention_backward_and_sums(
            qkv_t,
            g_t.reshape(heads, width, length),
            o_t,
            inverse,
            probs,
            normed_t,
            up_sum,
            out_sum,
            dp_size,
        )
        own, other, small, g_qkv, g_proj, g_down = token_gradients(
            d_qkv.reshape(-1, length),
            w_own,
            x_pair,
            grad_hidden,
            gain_attn,
            grad_gain_ffn,
            last,
            late,
            pooled,
            grad_proj,
            grad_block_all,
            every_act,
            diag_grads,
            bucket_count,
            dp_size,
        )
        g_query, g_key, g_value = g_qkv
        grad_tokens = jnp.stack(by_row(own, other.reshape(own.shape).astype(F32)))
        grad_gain_attn, grad_gain_ffn = small[:6].reshape(-1), small[6:12].reshape(-1)
        table_grad = small[12:, :bucket_count].T
    else:
        attended_t = heads_to_tokens(o_b.reshape(columns, length))
        hidden = x_own + jnp.einsum("ct,cd->td", attended_t, w_out, preferred_element_type=F32)
        normed_two = normed(hidden, gain_ffn).astype(BF16)
        up_proj = dot(normed_two, w_up)
        below = 0.5 * (1.0 + lax.erf(up_proj * (0.5**0.5)))
        act = (up_proj * below).astype(BF16)
        slope = (below + up_proj * jnp.exp(-0.5 * up_proj * up_proj) * 0.3989422804014327).astype(BF16)
        block_out = hidden + dot(act, w_down)
        mixed = hand_back(block_out.astype(BF16), BF16)
        member = (seg_own[None, :] == slot_ids[:, None]).astype(F32)
        sums = jnp.dot(member, block_out, precision=lax.Precision.HIGHEST)
        act_sums = dot(member.astype(BF16), act)

        loss, pooled, grad_proj, grad_block_all, every_act = loss_head(
            sums, act_sums, info, w_proj, dp_size, seq_size
        )
        grad_seg = lax.dynamic_slice_in_dim(grad_block_all, (dp_at * 2 + row) * slots, slots, 0)

        grad_act = dot_nt(grad_seg.astype(BF16), w_down)
        act_high = grad_act.astype(BF16)
        act_low = (grad_act - act_high.astype(F32)).astype(BF16)
        member_t = member.T.astype(BF16)
        spread = dot(
            jnp.concatenate([member_t, member_t], axis=1),
            jnp.concatenate([act_high, act_low], axis=0),
        )
        grad_up = (spread * slope.astype(F32)).astype(BF16)
        grad_wup = lax.dot_general(
            normed_two, grad_up, (((0,), (0,)), ((), ())), preferred_element_type=F32
        ).astype(BF16)
        grad_hidden, grad_gain_ffn = norm_back(hidden, gain_ffn, dot_nt(grad_up, w_up))
        grad_hidden = grad_hidden + jnp.dot(member.T, grad_seg, precision=lax.Precision.HIGHEST)
        grad_hidden_b = grad_hidden.astype(BF16)
        grad_wout = dot(attended_t, grad_hidden_b).astype(BF16)
        grad_att_t = dot_nt(w_out, grad_hidden_b).astype(BF16)
        g_t = tokens_to_heads(grad_att_t).reshape(heads, width, length)
        d_qkv, diag_grads = attention_backward(qkv_t, g_t, o_t, inverse, probs)
        every_act = every_act.reshape(-1, every_act.shape[2])
        proj_rows, proj_cols = model_width // dp_size, w_proj.shape[1] // seq_size
        g_proj = lax.dot_general(
            lax.dynamic_slice_in_dim(pooled, dp_at * proj_rows, proj_rows, 1),
            lax.dynamic_slice_in_dim(grad_proj, seq_at * proj_cols, proj_cols, 1),
            (((0,), (0,)), ((), ())),
            preferred_element_type=F32,
        )
        down_rows, down_cols = w_down.shape[0] // dp_size, model_width // seq_size
        g_down = lax.dot_general(
            every_act,
            lax.dynamic_slice_in_dim(grad_block_all, seq_at * down_cols, down_cols, 1)
            .astype(BF16)
            .astype(F32),
            (((0,), (0,)), ((), ())),
            precision=lax.Precision.HIGHEST,
        )
        table_part = jnp.einsum(
            "htx,txb->bh", diag_grads[:, :BANDS], onehot, precision=lax.Precision.HIGHEST
        )
        table_grad = jnp.zeros((bucket_count, head_count), F32)
        for block in range(blocks):
            table_grad = lax.dynamic_update_slice_in_dim(
                table_grad,
                table_part[:, block * block_heads : (block + 1) * block_heads],
                turn * block_heads,
                1,
            )
        def packed(gain_attn_part):
            small = jnp.concatenate([gain_attn_part, grad_gain_ffn, table_grad.reshape(-1)])
            return jnp.concatenate([small, jnp.zeros((-small.shape[0] % 1024,), F32)]).reshape(-1, 128)

        d_qkv = d_qkv.reshape(3 * columns, length)

        def owner_sum(value):
            value = lax.psum_scatter(value, "dp", scatter_dimension=0, tiled=True)
            return lax.psum_scatter(value, "seq", scatter_dimension=1, tiled=True).astype(F32)

        def own_columns(value):
            full = jnp.zeros((model_width, model_width), BF16)
            return lax.dynamic_update_slice_in_dim(full, value, turn * columns, 1)

        grad_w = lax.dot_general(
            normed_one, d_qkv, (((0,), (1,)), ((), ())), preferred_element_type=F32
        ).astype(BF16)
        grad_w = grad_w.reshape(model_width, heads, 3, width)
        g_query, g_key, g_value = [
            owner_sum(own_columns(grad_w[:, :, part].reshape(model_width, columns)))
            for part in range(3)
        ]
        g_up, g_out = owner_sum(grad_wup), owner_sum(grad_wout)
        grad_normed_part = jnp.einsum("ct,dc->td", d_qkv, w_qkv, preferred_element_type=F32)
        grad_normed = pieces_of(grad_normed_part, turn, 0)
        for step in range(1, half):
            send = pieces_of(grad_normed_part, lax.rem(turn + step, half), 0).astype(BF16)
            grad_normed = grad_normed + lax.ppermute(send, "seq", among(step)).astype(F32)
        grad_x, grad_gain_attn = norm_back(x_own, gain_attn, grad_normed)
        grad_tokens = hand_back(grad_hidden + grad_x, BF16)
        small = total_over_all(packed(grad_gain_attn), dp_size, seq_size)
        small = small.reshape(-1)
        grad_gain_attn, grad_gain_ffn = small[:model_width], small[model_width : 2 * model_width]
        table_grad = small[2 * model_width :][: bucket_count * head_count]
        table_grad = table_grad.reshape(bucket_count, head_count)
    return (
        mixed,
        loss[0, 0],
        grad_tokens,
        g_query,
        g_key,
        g_value,
        g_out,
        g_up,
        g_down,
        g_proj,
        grad_gain_attn,
        grad_gain_ffn,
        table_grad,
    )


def solution(mesh):
    in_specs = (P("dp", "seq", None), P("dp", "seq"), P("dp", None)) + (P(),) * 10
    out_specs = (
        (P("dp", "seq", None), P(), P("dp", "seq", None)) + (P("dp", "seq"),) * 7 + (P(),) * 3
    )
    return jax.shard_map(
        on_device, mesh=mesh, in_specs=in_specs, out_specs=out_specs, check_vma=False
    )
```

time: 1790 us -> 288 us (0.16)
  waiting for transfers between devices: 620 us -> 0 us
  matrix products: 613 us -> 0.16 us
  Pallas kernels: 0 us -> 275 us
  local copies, waits for them, and re-layouts: 241 us -> 7.79 us
  other arithmetic: 177 us -> 3.79 us
  blocking collectives: 109 us -> 0 us
    dot_general x45 -> x1, matrix products: 613 us -> 0.16 us  [on_device(): jnp.einsum('txb,bh->htx', onehot, table, precision=lax.Precision.HIGHEST)]
    reduce_scatter x11 -> x0, waiting for transfers between devices: 506 us -> none  [the longest x1 96.6 us: on_device(): lax.psum_scatter(grad_wup.astype(jnp.bfloat16), 'dp', scatter_dimension=0...]
    pallas_call x0 -> x5, Pallas kernels: none -> 275 us  [the longest x1 102 us: attention_backward_and_sums(): pl.pallas_call(functools.partial(backward_kernel, dp_size), grid=(heads,)...]
    convert_element_type x12 -> x0, other arithmetic: 116 us -> none  [the longest x2 80 us: query_side(): grad_scores = (weights * (grad_weights - centre)).astype(jnp.bfloat16)]
    unnamed x25 -> x0, waiting for transfers between devices: 113 us -> none
    convert_element_type x2 -> x0, local copies, waits for them, and re-layouts: 89.1 us -> none  [query_side(): grad_scores = (weights * (grad_weights - centre)).astype(jnp.bfloat16)]
    while x46 -> x0, local copies, waits for them, and re-layouts: 74.8 us -> none  [the longest x6 64.6 us: on_device(): lax.map(forward_step, (blocked(query_rows), blocked(keys_all), blocked(va...]
    all_gather x3 -> x0, blocking collectives: 58.1 us -> none  [the longest x1 31.1 us: on_device(): lax.all_gather(embed_b, 'dp', axis=0, tiled=True)]
  transfers between devices with their start and end apart: 19 -> 0, of which waited for: 15 -> 0; matrix products, arithmetic and copies ran while one was open for 44% -> 0% of each run, Pallas kernels for 0% -> 0%
where the time goes in v1:
time: 288 us; the launch traced here: 287 us
  Pallas kernels  275 us (95%)
  local copies, waits for them, and re-layouts  7.79 us (3%)
  other arithmetic  3.79 us (1%)
    pallas_call x1, Pallas kernels, attention_backward_and_sums(): pl.pallas_call(functools.partial(backward_kernel, dp_size), grid=(heads,)...  102 us
    pallas_call x1, Pallas kernels, feed_forward_and_loss(): pl.pallas_call(functools.partial(middle_kernel, dp_size), in_specs=[vmem]...  70.2 us
    pallas_call x1, Pallas kernels, attention_forward(): pl.pallas_call(functools.partial(forward_kernel, slots), grid=(heads,), i...  40.9 us
    pallas_call x1, Pallas kernels, token_gradients(): pl.pallas_call(functools.partial(tail_kernel, dp_size, buckets), in_specs...  32.5 us
    pallas_call x1, Pallas kernels, gather_and_project(): pl.pallas_call(front_kernel, in_specs=[vmem] * 4 + [anywhere] * 3, out_sp...  29.4 us

profile of v1, /device:TPU:0, one launch (start us, length us, event | category | flops | bytes accessed | tf_op | source)
XLA Modules:
  0.0 287.4 jit_solution(7016373689803999001)
XLA Ops:
  0.7 29.4 %gather_and_project.1 = (bf16[1152,2048]{1,0:T(8,128)(2,1)}, bf16[768,2048]{1,0:T(8,128)(2,1)}, bf16[1024,768]{1,0:T(8,128)(2,1)}, s32[8,2048]{1,0:T(8,128)}, bf...) custom-call(bf16[2,512,768]{2,1,0:T(8,128)(2,1)} %tokens_ref.1, s32[2,512]{1,0:T(2,128)} %seg_ref.1, ...), custom_call_target="tpu_custom_call" | custom-call | flops 3623878656 | bytes 20971520 | tf_op jit(solution)/shard_map/gather_and_project/pallas_call | solution.py:1089
  30.1 0.1 fusion.11
  30.2 0.2 fusion.2
  30.4 0.6 concatenate.7.diag_ref
  31.1 40.9 %attention_forward.1 = (f32[6,64,2048]{2,1,0:T(8,128)}, bf16[6,64,2048]{2,1,0:T(8,128)(2,1)}, f32[6,1,2048]{2,1,0:T(1,128)}, bf16[6,2048,2048]{2,1,0:T(8,128)(2,1)}) custom-call(bf16[6,3,64,2048]{3,2,1,0:T(8,128)(2,1)} %bitcast.28, bf16[6,3,64,2048]{3,2,1,0:T(8,128)(2,1)} %bitcast.29, bf16[6,3,64,2048]{3,2,1,0:T(8,128)(2,1)} %bitcast.30, ...), custom_call_target="tpu_custom_call" | custom-call | flops 12884901888 | bytes 59768832 | tf_op jit(solution)/shard_map/attention_forward/pallas_call | solution.py:207
  72.0 70.2 %feed_forward_and_loss.1 = (bf16[2,512,768]{2,1,0:T(8,128)(2,1)}, f32[8,128]{1,0:T(8,128)}, bf16[128,768]{1,0:T(8,128)(2,1)}, bf16[128,768]{1,0:T(8,128)(2,1)}, ...) custom-call(f32[8,128]{1,0:T(8,128)} %get-tuple-element.47.info_ref,, ...), custom_call_target="tpu_custom_call" | custom-call | flops 19327352832 | bytes 25165824 | tf_op jit(solution)/shard_map/feed_forward_and_loss/pallas_call | solution.py:1514
  142.2 1.2 slice.12
  143.4 101.8 %attention_backward_and_sums.1 = (bf16[6,3,64,2048]{3,2,1,0:T(8,128)(2,1)}, f32[6,8,256]{2,1,0:T(8,128)}, f32[96,768]{1,0:T(8,128)}, f32[96,192]{1,0:T(8,128)}, ...) custom-call(bf16[6,3,64,2048]{3,2,1,0:T(8,128)(2,1)} %bitcast.31, bf16[6,3,64,2048]{3,2,1,0:T(8,128)(2,1)} %bitcast.32, ...), custom_call_target="tpu_custom_call" | custom-call | flops 25769803776 | bytes 66060288 | tf_op jit(solution)/shard_map/attention_backward_and_sums/pallas_call | solution.py:634
  245.2 32.5 %token_gradients.1 = (f32[512,768]{1,0:T(8,128)}, bf16[4,128,768]{2,1,0:T(8,128)(2,1)}, f32[24,128]{1,0:T(8,128)}, f32[3,96,192]{2,1,0:T(8,128)}, f32[96,192]{1,0:T(8,128)}, /*index=5*/f32[384,192]{1,0:T(8,128)}) custom-call(f32[768]{0:T(1024)} %gain_ref.5, f32[8,768]{1,0:T(8,128)} %get-tuple-element.55.ffn_ref, ...), custom_call_target="tpu_custom_call" | custom-call | flops 3623878656 | bytes 16777216 | tf_op jit(solution)/shard_map/token_gradients/pallas_call | solution.py:1819
  277.7 1.8 fusion
  279.6 0.0 copy-start.3
  279.6 0.0 copy-start.1
  279.6 0.0 copy-start.6
  279.6 0.0 copy-start
  279.6 1.9 pad_maximum_fusion
  281.5 0.7 slice_bitcast_fusion
  282.2 0.9 copy.27
  283.1 0.0 copy-done.6
  283.1 0.6 slice_bitcast_fusion.4
  283.7 0.6 slice_bitcast_fusion.3
  284.3 1.1 copy.32
  285.4 0.6 copy.33
  286.1 0.7 copy.34
  286.8 0.6 copy.35
  (15 shorter events, 0.1 us)
Async XLA Ops:
  0.6 29.6 %copy-start.7 = (f32[32,12]{0,1:T(8,128)S(1)}, f32[32,12]{0,1:T(8,128)}, u32[]{:S(2)}) copy-start(f32[32,12]{0,1:T(8,128)} %param.25) | copy-start | bytes 4612
  279.6 1.9 copy-start.3
  279.6 2.6 copy-start.1
  279.6 3.5 %copy-start.6 = (f32[24,128]{1,0:T(8,128)S(1)}, f32[24,128]{1,0:T(8,128)}, u32[]{:S(2)}) copy-start(f32[24,128]{1,0:T(8,128)} %get-tuple-element.80) | copy-start | bytes 36868
  279.6 4.7 %copy-start = (bf16[2,512,768]{2,1,0:T(8,128)(2,1)S(1)}, bf16[2,512,768]{2,1,0:T(8,128)(2,1)}, u32[]{:S(2)}) copy-start(bf16[2,512,768]{2,1,0:T(8,128)(2,1)} %get-tuple-element.116) | copy-start | bytes 4718596
  284.3 1.2 copy-start.4
  284.3 1.8 copy-start.2
  284.3 2.5 copy-start.5

commit v2 on v1

--- a/solution.py
+++ b/solution.py
@@ -141,57 +141,61 @@
         part = tile_part(tile)
         return extended(q_ref[0, 0, :, part], segment_rows(seg_ref[0:1, part], slots, 0.0, MASKED), [])
 
+    def far_bias(chunk, tile):
+        return jnp.where(chunk > tile, after, before)
+
     def score(span, tile, qx, top):
         products = dot(kx[span_part(span, tile), :], qx)
         for sub in range(SPAN // TILE):
             turn = span * (SPAN // TILE) + sub
             chunk = chunk_at(tile, turn, count)
+            scores = products[sub * TILE : (sub + 1) * TILE]
+            if not is_far(turn, count):
+                scores = scores + bias[band_of(chunk, tile)]
+            held[turn] = scores
+            best = jnp.max(scores.reshape(TILE // 8, 8, TILE), axis=0)
             if is_far(turn, count):
-                added = jnp.where(chunk > tile, after, before)
-            else:
-                added = bias[band_of(chunk, tile)]
-            scores = products[sub * TILE : (sub + 1) * TILE] + added
-            held[turn] = scores
-            top = jnp.maximum(top, jnp.max(scores.reshape(TILE // 8, 8, TILE), axis=0))
+                best = best + far_bias(chunk, tile)
+            top = jnp.maximum(top, best)
         return top
 
-    def weigh(turn, tile, top, total, out):
-        chunk = tile_part(chunk_at(tile, turn, count))
-        weights = jnp.exp(held[turn] - top)
-        total = total + jnp.sum(weights.reshape(TILE // 8, 8, TILE), axis=0)
-        weights = weights.astype(BF16)
-        p_ref[0, chunk, tile_part(tile)] = weights
-        return total, out + dot(v_ref[0, 0, :, chunk], weights)
-
-    def finish(tile, total, out):
+    def weigh(turn, tile, top, out):
+        chunk = chunk_at(tile, turn, count)
+        shift = top - far_bias(chunk, tile) if is_far(turn, count) else top
+        weights = jnp.exp(held[turn] - shift).astype(BF16)
+        p_ref[0, tile_part(chunk), tile_part(tile)] = weights
+        values = jnp.concatenate([v_ref[0, 0, :, tile_part(chunk)], jnp.ones((16, TILE), BF16)], axis=0)
+        return out + dot(values, weights)
+
+    def finish(tile, out):
         part = tile_part(tile)
-        inverse = 1.0 / jnp.sum(total, axis=0, keepdims=True)
-        out = out * inverse
+        inverse = 1.0 / out[width : width + 1]
+        out = out[:width] * inverse
         o_ref[0, :, part] = out
         ob_ref[0, :, part] = out.astype(BF16)
         inv_ref[0, :, part] = inverse
 
+    width = v_ref.shape[2]
     lowest = jnp.full((8, TILE), -jnp.inf, F32)
-    start = (jnp.zeros((8, TILE), F32), jnp.zeros((v_ref.shape[2], TILE), F32))
+    start = jnp.zeros((width + 16, TILE), F32)
 
     def body(tile, top):
-        qx, following = query_side(tile + 1), lowest
-        total, out = start
+        qx, following, out = query_side(tile + 1), lowest, start
         for span in range(spans):
             for turn in range(span * (SPAN // TILE), (span + 1) * (SPAN // TILE)):
-                total, out = weigh(turn, tile, top, total, out)
+                out = weigh(turn, tile, top, out)
             following = score(span, tile + 1, qx, following)
-        finish(tile, total, out)
+        finish(tile, out)
         return jnp.max(following, axis=0, keepdims=True)
 
     qx, top = query_side(0), lowest
     for span in range(spans):
         top = score(span, 0, qx, top)
     top = lax.fori_loop(0, count - 1, body, jnp.max(top, axis=0, keepdims=True))
-    total, out = start
+    out = start
     for turn in range(count):
-        total, out = weigh(turn, count - 1, top, total, out)
-    finish(count - 1, total, out)
+        out = weigh(turn, count - 1, top, out)
+    finish(count - 1, out)
 
 
 def head_spec(rows, length):
@@ -277,7 +281,6 @@
     dkv,
     gx,
     both,
-    weighed,
     left,
     beside=None,
 ):
@@ -312,44 +315,46 @@
         lower = jnp.transpose(jnp.concatenate([nothing, grad.astype(F32)], axis=0))
         both[slot] = jnp.concatenate([upper, lower], axis=0).astype(BF16)
 
-    def weigh(tile, span, slot):
-        weighed[span] = dot(vx[span_part(span, tile), :], gx[slot])
-
-    def score(tile, span):
+    def score(tile, span, slot):
+        products = dot(vx[span_part(span, tile), :], gx[slot])
         for sub in range(subs):
             turn, rows = span * subs + sub, pl.ds(sub * TILE, TILE)
             chunk = chunk_at(tile, turn, count)
             weights = p_ref[0, tile_part(chunk), tile_part(tile)]
-            grad_scores = weights.astype(F32) * weighed[span, rows, :]
-            if is_far(turn, count):
-                side = (chunk > tile).astype(jnp.int32)
-                far[side] += jnp.sum(grad_scores.reshape(TILE // 8, 8, TILE), axis=0)
-            else:
-                sums[band_of(chunk, tile)] += grad_scores
-            left[span, rows, :TILE] = grad_scores.astype(BF16)
+            grad_scores = weights * products[sub * TILE : (sub + 1) * TILE].astype(BF16)
+            if not is_far(turn, count):
+                sums[band_of(chunk, tile)] += grad_scores.astype(F32)
+            left[span, rows, :TILE] = grad_scores
             left[span, rows, TILE:] = weights
 
     def gather(tile, span, slot, grad_query):
         products = dot(left[span], both[slot])
+        row = lax.broadcasted_iota(jnp.int32, (16, TILE), 0)
         for sub in range(subs):
-            part = tile_part(chunk_at(tile, span * subs + sub, count))
+            turn = span * subs + sub
+            chunk = chunk_at(tile, turn, count)
+            part = tile_part(chunk)
             rows = slice(sub * TILE, (sub + 1) * TILE)
             dkv[part, :] += products[rows]
-            grad_query = grad_query + dot(k_ref[0, 0, :, part], left[span, rows, :TILE])
+            marks = jnp.zeros((16, TILE), F32)
+            if is_far(turn, count):
+                marks = jnp.where(row == jnp.where(chunk > tile, 1, 0), 1.0, 0.0)
+            keys = jnp.concatenate([k_ref[0, 0, :, part], marks.astype(BF16)], axis=0)
+            grad_query = grad_query + dot(keys, left[span, rows, :TILE])
         return grad_query
 
     def store(tile, grad_query):
-        d_ref[0, 0, :, tile_part(tile)] = grad_query.astype(BF16)
-
-    empty = jnp.zeros((width, TILE), F32)
+        d_ref[0, 0, :, tile_part(tile)] = grad_query[:width].astype(BF16)
+
+    empty = jnp.zeros((width + 16, TILE), F32)
 
     def step(tile, slot, following, behind, grad_behind):
-        weigh(tile, 1, slot)
-        score(tile, 0)
-        store(behind, gather(behind, 1, 1 - slot, grad_behind))
+        score(tile, 0, slot)
+        grad_behind = gather(behind, 1, 1 - slot, grad_behind)
+        store(behind, grad_behind)
+        far[...] += grad_behind[width : width + 8]
         queries_side(following, 1 - slot)
-        weigh(following, 0, 1 - slot)
-        score(tile, 1)
+        score(tile, 1, slot)
         return gather(tile, 0, slot, empty)
 
     def one(tile, carried):
@@ -359,9 +364,10 @@
         return step(tile, slot, lax.rem(tile + 1, count), lax.rem(tile + count - 1, count), carried)
 
     queries_side(0, 0)
-    weigh(0, 0, 0)
     carried = lax.fori_loop(0, count, one, empty)
-    store(count - 1, gather(count - 1, 1, 1, carried))
+    grad_last = gather(count - 1, 1, (count - 1) % 2, carried)
+    store(count - 1, grad_last)
+    far[...] += grad_last[width : width + 8]
     d_both = jnp.transpose(dkv[...])
     d_ref[0, 1] = d_both[:width].astype(BF16)
     d_ref[0, 2] = d_both[width:].astype(BF16)
@@ -374,8 +380,8 @@
             totals[row] = block if totals[row] is None else totals[row] + block
     for row, total in enumerate(totals):
         if row in (0, BANDS - 1):
-            more = far[min(row, 1)]
-            total = jnp.sum(total + more[:, :BLOCK] + more[:, BLOCK:], axis=0, keepdims=True)
+            more = far[min(row, 1) : min(row, 1) + 1, :]
+            total = jnp.sum(total, axis=0, keepdims=True) + more[:, :BLOCK] + more[:, BLOCK:]
             total = jnp.concatenate([total, jnp.zeros_like(total)], axis=1)
         else:
             total = diagonal_sums(total)
@@ -411,7 +417,6 @@
     dkv,
     gx,
     both,
-    weighed,
     left,
     up_near,
     out_near,
@@ -500,7 +505,6 @@
         dkv,
         gx,
         both,
-        weighed,
         left,
         beside,
     )
@@ -565,11 +569,10 @@
         scratch_shapes=[
             pltpu.VMEM((2 * length, 128), BF16),
             pltpu.VMEM((BANDS, TILE, TILE), F32),
-            pltpu.VMEM((2, 8, TILE), F32),
+            pltpu.VMEM((8, TILE), F32),
             pltpu.VMEM((length, 128), F32),
             pltpu.VMEM((2, 128, TILE), BF16),
             pltpu.VMEM((2, 2 * TILE, 128), BF16),
-            pltpu.VMEM((2, SPAN, TILE), F32),
             pltpu.VMEM((2, SPAN, 2 * TILE), BF16),
         ],
     )
@@ -1168,6 +1171,7 @@
     act,
     slope,
     total,
+    raw,
     members_t,
     sum_parts,
     mixed_out,
@@ -1285,17 +1289,27 @@
     each(0, tokens // TILE, attended_tile)
     loads[2].wait()
 
-    def up(at):
+    def up(at, slot):
+        raw[slot] = dot(normed_two[...], w_up[:, tile_part(at)])
+
+    def bend(at, slot):
         lanes = tile_part(at)
-        for half in range(2):
-            rows = half_of(half)
-            value = dot(normed_two[rows, :], w_up[:, lanes])
-            below = 0.5 + 0.5 * lax.erf(value * (0.5**0.5))
-            density = jnp.exp(-0.5 * value * value) * 0.3989422804014327
-            act[rows, lanes] = (value * below).astype(BF16)
-            slope[rows, lanes] = (below + value * density).astype(BF16)
-
-    each(0, units // TILE, up)
+        value = raw[slot]
+        below = 0.5 + 0.5 * lax.erf(value * (0.5**0.5))
+        density = jnp.exp(-0.5 * value * value) * 0.3989422804014327
+        act[:, lanes] = (value * below).astype(BF16)
+        slope[:, lanes] = (below + value * density).astype(BF16)
+
+    strips = units // TILE
+
+    def two_strips(at):
+        up(2 * at + 1, 1)
+        bend(2 * at, 0)
+        up(lax.rem(2 * at + 2, strips), 0)
+        bend(2 * at + 1, 1)
+
+    up(0, 0)
+    each(0, strips // 2, two_strips)
     loads[3].wait()
     member = jnp.transpose(members(pl.ds(0, tokens), 1))[:16].astype(BF16)
     sum_parts[...] = jnp.zeros_like(sum_parts)
@@ -1517,7 +1531,7 @@
         out_specs=[vmem] * 7 + [anywhere] + [vmem] * 3,
         out_shape=[
             shape((2, piece, model), BF16),
-            shape((8, 128), F32),
+            shape((1, 1), F32),
             shape((many, model), BF16),
             shape((many, w_proj.shape[1]), BF16),
             shape((many, model), F32),
@@ -1541,6 +1555,7 @@
             pltpu.VMEM((tokens, units), BF16),
             pltpu.VMEM((tokens, units), BF16),
             pltpu.VMEM((tokens, model), F32),
+            pltpu.VMEM((2, tokens, TILE), F32),
             pltpu.VMEM((16, tokens), BF16),
             pltpu.VMEM((16, model), F32),
             pltpu.VMEM((piece, model), BF16),
@@ -1681,7 +1696,7 @@
     gain = gain_ref[...].reshape(1, model)
     loads[0].wait()
     loads[1].wait()
-    def quarter(at):
+    def send_near(at):
         near_out[at] = product(1 - turn, at).astype(BF16)
 
         @pl.when(at == 0)
@@ -1689,6 +1704,8 @@
             pl.semaphore_wait(barrier, seq_size - 1 + dp_size - 1)
 
         near_copy(at).start()
+
+    def quarter(at):
         part[...] = product(turn, at)
 
         @pl.when(at == 0)
@@ -1696,6 +1713,10 @@
             each(1, dp_size, lambda step: last_copy(step, dp_at).start())
             loads[2].wait()
             loads[3].wait()
+
+        @pl.when(at < 3)
+        def _():
+            send_near(at + 1)
 
         near_copy(at).wait_recv()
         which = jnp.where(at < 2, 1 - row, row)
@@ -1723,6 +1744,7 @@
 
         each(0, parts, block)
 
+    each(0, 1, send_near)
     each(0, 4, quarter)
 
     heads = diag_ref.shape[0]
@@ -1785,7 +1807,7 @@
     block = turned[2, own_cols, :].astype(BF16)
     high = act.astype(BF16)
     rest = (act - high.astype(F32)).astype(BF16)
-    g_down_ref[...] = dot_nt(high, block) + dot_nt(rest, block)
+    g_down_ref[...] = dot_nt(block, high) + dot_nt(block, rest)
 
     each(1, dp_size, lambda step: last_copy(step, lax.rem(dp_at + step, dp_size)).wait_recv())
     last_far[dp_at] = jnp.zeros(last_far.shape[1:], BF16)
@@ -1826,7 +1848,7 @@
             shape((24, 128), F32),
             shape((3, rows, run * width), F32),
             shape((rows, out_cols), F32),
-            shape((act.shape[2], out_cols), F32),
+            shape((out_cols, act.shape[2]), F32),
         ],
         scratch_shapes=[
             pltpu.VMEM(w_qkv.shape, BF16),
@@ -1880,6 +1902,45 @@
     )
 
 
+def finish_kernel(own_ref, other_ref, small_ref, *refs):
+    sources, (tokens_ref, attn_ref, ffn_ref, table_ref), targets = refs[:6], refs[6:10], refs[10:]
+    lanes = attn_ref.shape[0] // 128
+    for first, target in ((0, attn_ref), (lanes, ffn_ref)):
+        parts = [small_ref[first + at : first + at + 1, :] for at in range(lanes)]
+        target[...] = jnp.concatenate(parts, axis=1).reshape(target.shape)
+    table_ref[...] = small_ref[2 * lanes : 2 * lanes + table_ref.shape[0], : table_ref.shape[1]]
+    row = lax.axis_index("seq") // 2
+    tokens_ref[row] = own_ref[...]
+
+    def widen(at):
+        rows = pl.ds(pl.multiple_of(at * BLOCK, BLOCK), BLOCK)
+        tokens_ref[1 - row, rows, :] = other_ref[at].astype(F32)
+
+    each(0, other_ref.shape[0], widen)
+    for kind in range(3):
+        targets[kind][...] = sources[0][kind]
+    for source, target in zip(sources[1:], targets[3:]):
+        target[...] = source[...]
+
+
+def finish(own, other, small, table_shape, g_qkv, *rest):
+    piece, model = own.shape
+    vmem = pl.BlockSpec(memory_space=pltpu.VMEM)
+    shape = lambda like: jax.ShapeDtypeStruct(like.shape, like.dtype)
+    return pl.pallas_call(
+        finish_kernel,
+        in_specs=[vmem] * (4 + len(rest)),
+        out_specs=[vmem] * (7 + len(rest)),
+        out_shape=[jax.ShapeDtypeStruct((2, piece, model), F32)]
+        + [jax.ShapeDtypeStruct((model,), F32)] * 2
+        + [jax.ShapeDtypeStruct(table_shape, F32)]
+        + [jax.ShapeDtypeStruct(g_qkv.shape[1:], F32)] * 3
+        + [shape(value) for value in rest],
+        compiler_params=pltpu.CompilerParams(vmem_limit_bytes=60 * MIB),
+        name="finish",
+    )(own, other, small, g_qkv, *rest)
+
+
 def normed(inputs, gain_vec):
     return inputs * lax.rsqrt(jnp.mean(inputs * inputs, axis=-1, keepdims=True) + EPS) * gain_vec
 
@@ -2061,10 +2122,23 @@
             bucket_count,
             dp_size,
         )
-        g_query, g_key, g_value = g_qkv
-        grad_tokens = jnp.stack(by_row(own, other.reshape(own.shape).astype(F32)))
-        grad_gain_attn, grad_gain_ffn = small[:6].reshape(-1), small[6:12].reshape(-1)
-        table_grad = small[12:, :bucket_count].T
+        (
+            grad_tokens,
+            grad_gain_attn,
+            grad_gain_ffn,
+            table_grad,
+            g_query,
+            g_key,
+            g_value,
+            mixed,
+            g_up,
+            g_out,
+            g_proj,
+            g_down,
+        ) = finish(
+            own, other, small, (head_count, bucket_count), g_qkv, mixed, g_up, g_out, g_proj, g_down
+        )
+        g_down, table_grad = g_down.T, table_grad.T
     else:
         attended_t = heads_to_tokens(o_b.reshape(columns, length))
         hidden = x_own + jnp.einsum("ct,cd->td", attended_t, w_out, preferred_element_type=F32)

time: 288 us -> 279 us (0.969)
  local copies, waits for them, and re-layouts: 7.79 us -> 1.43 us
  other arithmetic: 3.79 us -> 0.09 us
    pallas_call x1, Pallas kernels: 102 us -> 96.2 us  [attention_backward_and_sums(): pl.pallas_call(functools.partial(backward_kernel, dp_size), grid=(heads,)...]
    pallas_call x0 -> x1, Pallas kernels: none -> 5.17 us  [finish(): pl.pallas_call(finish_kernel, in_specs=[vmem] * (4 + len(rest)), out_spec...]
    unnamed x21 -> x0, local copies, waits for them, and re-layouts: 4.04 us -> none
    another operation x2 -> x0, other arithmetic: 3.7 us -> none  [on_device(): grad_tokens = jnp.stack(by_row(own, other.reshape(own.shape).astype(F32)))]
where the time goes in v2:
time: 279 us; the launch traced here: 278 us
  Pallas kernels  274 us (98%)
    pallas_call x1, Pallas kernels, attention_backward_and_sums(): pl.pallas_call(functools.partial(backward_kernel, dp_size), grid=(heads,)...  96.2 us
    pallas_call x1, Pallas kernels, feed_forward_and_loss(): pl.pallas_call(functools.partial(middle_kernel, dp_size), in_specs=[vmem]...  70.3 us
    pallas_call x1, Pallas kernels, attention_forward(): pl.pallas_call(functools.partial(forward_kernel, slots), grid=(heads,), i...  38.6 us
    pallas_call x1, Pallas kernels, token_gradients(): pl.pallas_call(functools.partial(tail_kernel, dp_size, buckets), in_specs...  34.4 us
    pallas_call x1, Pallas kernels, gather_and_project(): pl.pallas_call(front_kernel, in_specs=[vmem] * 4 + [anywhere] * 3, out_sp...  29.4 us

profile of v2, /device:TPU:0, one launch (start us, length us, event | category | flops | bytes accessed | tf_op | source)
XLA Modules:
  0.0 278.3 jit_solution(8912049833160536498)
XLA Ops:
  0.7 0.8 constant_dynamic-slice_fusion.1
  1.5 0.1 fusion.9
  1.6 0.2 fusion
  1.8 0.6 concatenate.7.diag_ref
  2.4 29.4 %gather_and_project.1 = (bf16[1152,2048]{1,0:T(8,128)(2,1)}, bf16[768,2048]{1,0:T(8,128)(2,1)}, bf16[1024,768]{1,0:T(8,128)(2,1)}, s32[8,2048]{1,0:T(8,128)}, bf...) custom-call(bf16[2,512,768]{2,1,0:T(8,128)(2,1)} %tokens_ref.1, s32[2,512]{1,0:T(2,128)} %seg_ref.1, ...), custom_call_target="tpu_custom_call" | custom-call | flops 3623878656 | bytes 20971520 | tf_op jit(solution)/shard_map/gather_and_project/pallas_call | solution.py:1092
  31.8 38.6 %attention_forward.1 = (f32[6,64,2048]{2,1,0:T(8,128)}, bf16[6,64,2048]{2,1,0:T(8,128)(2,1)}, f32[6,1,2048]{2,1,0:T(1,128)}, bf16[6,2048,2048]{2,1,0:T(8,128)(2,1)}) custom-call(bf16[6,3,64,2048]{3,2,1,0:T(8,128)(2,1)} %bitcast.12, bf16[6,3,64,2048]{3,2,1,0:T(8,128)(2,1)} %bitcast.13, bf16[6,3,64,2048]{3,2,1,0:T(8,128)(2,1)} %bitcast.14, ...), custom_call_target="tpu_custom_call" | custom-call | flops 12884901888 | bytes 59768832 | tf_op jit(solution)/shard_map/attention_forward/pallas_call | solution.py:211
  70.5 70.3 %feed_forward_and_loss.1 = (bf16[2,512,768]{2,1,0:T(8,128)(2,1)}, f32[1,1]{1,0:T(1,128)}, bf16[128,768]{1,0:T(8,128)(2,1)}, bf16[128,768]{1,0:T(8,128)(2,1)}, f3...) custom-call(f32[8,128]{1,0:T(8,128)} %get-tuple-element.59.info_ref,, ...), custom_call_target="tpu_custom_call" | custom-call | flops 19327352832 | bytes 25165824 | tf_op jit(solution)/shard_map/feed_forward_and_loss/pallas_call | solution.py:1528
  140.8 96.2 %attention_backward_and_sums.1 = (bf16[6,3,64,2048]{3,2,1,0:T(8,128)(2,1)}, f32[6,8,256]{2,1,0:T(8,128)}, f32[96,768]{1,0:T(8,128)}, f32[96,192]{1,0:T(8,128)}, ...) custom-call(bf16[6,3,64,2048]{3,2,1,0:T(8,128)(2,1)} %bitcast.15, bf16[6,3,64,2048]{3,2,1,0:T(8,128)(2,1)} %bitcast.16, ...), custom_call_target="tpu_custom_call" | custom-call | flops 25769803776 | bytes 66060288 | tf_op jit(solution)/shard_map/attention_backward_and_sums/pallas_call | solution.py:637
  236.9 34.4 %token_gradients.1 = (f32[512,768]{1,0:T(8,128)}, bf16[4,128,768]{2,1,0:T(8,128)(2,1)}, f32[24,128]{1,0:T(8,128)}, f32[3,96,192]{2,1,0:T(8,128)}, f32[96,192]{1,0:T(8,128)}, /*index=5*/f32[192,384]{1,0:T(8,128)}) custom-call(f32[768]{0:T(1024)} %gain_ref.5, f32[8,768]{1,0:T(8,128)} %get-tuple-element.65.ffn_ref, ...), custom_call_target="tpu_custom_call" | custom-call | flops 3623878656 | bytes 16777216 | tf_op jit(solution)/shard_map/token_gradients/pallas_call | solution.py:1841
  271.3 5.2 %finish.1 = (f32[2,512,768]{2,1,0:T(8,128)}, f32[768]{0:T(1024)}, f32[768]{0:T(1024)}, f32[12,32]{1,0:T(8,128)}, f32[96,192]{1,0:T(8,128)}, /*index=5*/f32[96,19...) custom-call(f32[512,768]{1,0:T(8,128)} %get-tuple-element.83.own_ref, ...), custom_call_target="tpu_custom_call" | custom-call | tf_op jit(solution)/shard_map/finish/pallas_call | solution.py:1930
  (3 shorter events, 0.0 us)
